TPU v7x, 32 devices: a whole 2x2x4 slice. The times are simulated.
32 devices in a mesh: ens: 2 (over x), lon: 16 (over z, y, core).
Axes of the slice: x: 2, y: 2, z: 4, core: 2. Of those that a mesh axis runs over, the one named last changes fastest.
Arguments:
- state: float32 [192, 768, 256], P('ens', 'lon'), parts along dimension 0, may hold values from -6 to 6
- courant: float32 [192, 768, 128], P('ens', 'lon'), parts along dimension 0, may hold values from -0.45 to 0.45
- daylit: int32 [192, 768], P('ens', 'lon'), parts along dimension 0, may hold values from 0 to 1, as said below
- insolation: float32 [192, 768], P('ens', 'lon'), parts along dimension 0, may hold values from 0.1 to 1
- long_in: bfloat16 [256, 1024], replicated, may hold values from -0.375 to 0.375
- long_out: bfloat16 [1024, 256], replicated, may hold values from -0.1875 to 0.1875
- short_in: bfloat16 [256, 1024], replicated, may hold values from -0.375 to 0.375
- short_sun: bfloat16 [1024], replicated, may hold values from -4 to 4
- short_mid: bfloat16 [2, 1024, 1024], replicated, may hold values from -0.1875 to 0.1875
- short_out: bfloat16 [1024, 256], replicated, may hold values from -0.1875 to 0.1875
Outputs:
- new_state: float32 [192, 768, 256], P('ens', 'lon'), parts along dimension 0
- tendency: bfloat16 [192, 768, 256], P('ens', 'lon'), parts along dimension 0
There are 2 independent parts, one for each index of `ens`. A program takes and returns all parts, laid end to end along the dimension named above; an argument that names none is the same for every part. Nothing has to cross between parts.
Inputs may be any that keep to these rules, and one draw needn't show every extreme that they name: In each latitude row the daylit columns are exactly 384 consecutive longitudes of the periodic circle, and the first of them lies within 48 longitudes of a point common to all rows of the part.
All inputs are finite; a program needn't handle non-finite values.
Results may differ from a plain program's by a relative error of at most 0.006.
Values may be sent and summed in bfloat16 or wider, within the bound.
No kernel may reach another device: no remote copies, remote signals or barrier semaphores. Data moves between devices by JAX's collectives and lax.ppermute only.
A program may use at most 128 MiB of HBM per device.

v0:
```python
import jax
import jax.numpy as jnp
from jax import lax
from jax.sharding import PartitionSpec as P


def padded_2(shard, sides, width):
    for axis, dim in sides:
        size, length = (lax.axis_size(axis), shard.shape[dim])
        up = [(i, (i + 1) % size) for i in range(size)]
        down = [(j, i) for i, j in up]
        last = lax.slice_in_dim(shard, length - width, length, axis=dim)
        leading = lax.slice_in_dim(shard, 0, width, axis=dim)
        before = lax.ppermute(last, axis, up)
        after = lax.ppermute(leading, axis, down)
        shard = jnp.concatenate([before, shard, after], axis=dim)
    return shard


def long_net(columns, long_in, long_out):
    hidden = jax.nn.silu(jnp.dot(columns, long_in, preferred_element_type=jnp.float32)).astype(
        jnp.bfloat16
    )
    return jnp.dot(hidden, long_out, preferred_element_type=jnp.float32)


def short_net(columns, sunlight, short_in, short_sun, short_mid, short_out):
    first = jnp.dot(columns, short_in, preferred_element_type=jnp.float32)
    first = first + sunlight[:, None] * short_sun.astype(jnp.float32)[None, :]
    hidden = jax.nn.silu(first).astype(jnp.bfloat16)
    hidden = jax.nn.silu(jnp.dot(hidden, short_mid[0], preferred_element_type=jnp.float32)).astype(
        jnp.bfloat16
    )
    hidden = jax.nn.silu(jnp.dot(hidden, short_mid[1], preferred_element_type=jnp.float32)).astype(
        jnp.bfloat16
    )
    return jnp.dot(hidden, short_out, preferred_element_type=jnp.float32).astype(jnp.bfloat16)


def advect(padded_state, padded_courant):
    courant_pair = jnp.concatenate([padded_courant, padded_courant], axis=-1)[:, :-1]
    east_flux = (
        jnp.maximum(courant_pair, 0.0) * padded_state[:, :-1]
        + jnp.minimum(courant_pair, 0.0) * padded_state[:, 1:]
    )
    return padded_state[:, 1:-1] - (east_flux[:, 1:] - east_flux[:, :-1])


def shards(
    state, courant, daylit, insolation, long_in, long_out, short_in, short_sun, short_mid, short_out
):
    lat_rows, lon_cells, features = state.shape
    column_count = lat_rows * lon_cells
    columns = state.reshape(column_count, features).astype(jnp.bfloat16)
    long_tend = long_net(columns, long_in, long_out)
    lit_mask = daylit.reshape(column_count)
    sunlight = insolation.reshape(column_count)
    short_cols = short_net(columns, sunlight, short_in, short_sun, short_mid, short_out)
    physics = long_tend + lit_mask[:, None].astype(jnp.float32) * short_cols.astype(jnp.float32)
    physics_grid = physics.reshape(lat_rows, lon_cells, features)
    tendency = physics_grid.astype(jnp.bfloat16)
    provisional = state + physics_grid
    padded = padded_2(
        jnp.concatenate([provisional, courant], axis=-1).astype(jnp.bfloat16), (("lon", 1),), 1
    ).astype(jnp.float32)
    padded_state = padded[:, :, :features]
    padded_courant = padded[:, :, features:]
    new_state = advect(padded_state, padded_courant)
    return (new_state, tendency)


def solution(mesh):
    in_specs = (
        P("ens", "lon", None),
        P("ens", "lon", None),
        P("ens", "lon"),
        P("ens", "lon"),
        P(),
        P(),
        P(),
        P(),
        P(),
        P(),
    )
    out_specs = (P("ens", "lon", None), P("ens", "lon", None))
    return jax.shard_map(shards, mesh=mesh, in_specs=in_specs, out_specs=out_specs, check_vma=False)
```

profile of v0, /device:TPU:0, one launch (start us, length us, event | category | flops | bytes accessed | tf_op | source)
XLA Modules:
  0.0 83.5 jit_solution(2287469324770430145)
XLA Ops:
  0.6 0.0 copy-start
  0.6 0.0 copy-start.5
  0.7 0.0 copy-start.6
  0.7 2.7 %convert_element_type.45 = bf16[96,48,256]{2,1,0:T(8,128)(2,1)S(1)} convert(f32[96,48,256]{2,1,0:T(8,128)} %param.10) | non-fusion elementwise | flops 1179648 | bytes 7077888 | tf_op jit(solution)/shard_map/convert_element_type | solution.py:54
  3.3 0.0 copy-done.5
  3.4 0.1 copy.13
  3.4 0.1 mul.44
  3.5 0.0 copy-done.6
  3.6 0.0 copy-done
  3.6 20.6 %fusion.13 = f32[4608,1024]{1,0:T(8,128)} fusion(bf16[4608,256]{1,0:T(8,128)(2,1)S(1)} %bitcast.16, bf16[256,1024]{1,0:T(8,128)(2,1)S(1)} %copy-done, f32[1024]{0:T(1024)S(1)} %convert_element_type.50, f32[4608]{0:T(1024)S(1)} %mul.44, bf16[2,1024,1024]{2,1,0:T(8,128)(2,1)} %param.18), kind=kOutput, calls=%fused_computation.21 | convolution fusion | flops 12112625664 | bytes 23877632 | tf_op jit(solution)/shard_map/dot_general | solution.py:31
  24.2 18.5 %fusion = f32[4608,1024]{1,0:T(8,128)} fusion(f32[4608,1024]{1,0:T(8,128)} %fusion.13, bf16[2,1024,1024]{2,1,0:T(8,128)(2,1)} %param.18), kind=kOutput, calls=%fused_computation.4 | convolution fusion | flops 9687269376 | bytes 39845888 | tf_op jit(solution)/shard_map/dot_general | solution.py:34
  42.7 0.0 copy-done.4
  42.7 0.1 copy.12
  42.8 0.1 convert_element_type.49
  42.9 0.0 copy-done.7
  42.9 10.6 %fusion.6 = f32[4608,256]{1,0:T(8,128)} fusion(bf16[1024,256]{1,0:T(8,128)(2,1)S(1)} %copy-done.7, f32[4608,1024]{1,0:T(8,128)} %fusion, f32[4608]{0:T(1024)S(1)} %convert_element_type.49), kind=kOutput, calls=%fused_computation.10 | convolution fusion | flops 2443051008 | bytes 24135680 | tf_op jit(solution)/shard_map/dot_general | solution.py:37
  53.5 8.8 %fusion.3 = f32[4608,256]{1,0:T(8,128)} fusion(f32[4608,256]{1,0:T(8,128)} %fusion.6, bf16[1024,256]{1,0:T(8,128)(2,1)} %param.15, bf16[4608,256]{1,0:T(8,128)(2,1)S(1)} %bitcast.17, bf16[256,1024]{1,0:T(8,128)(2,1)} %param.14), kind=kOutput, calls=%fused_computation.7 | convolution fusion | flops 4856610816 | bytes 12845056 | tf_op jit(solution)/shard_map/dot_general | solution.py:24
  62.3 4.7 %add_convert_fusion = bf16[96,48,256]{2,1,0:T(8,128)(2,1)S(1)} fusion(f32[96,48,256]{2,1,0:T(8,128)} %param.10, f32[96,48,256]{2,1,0:T(8,128)} %bitcast.14), kind=kLoop, calls=%fused_computation.20 | loop fusion | flops 2359296 | bytes 11796480 | tf_op jit(solution)/shard_map/convert
  67.0 0.0 copy-done.3
  67.1 0.0 copy-start.2
  67.1 0.2 convert.7
  67.2 0.3 pad_maximum_fusion.2
  67.5 0.5 collective-permute-start
  68.0 5.1 %collective-permute-start.1 = (bf16[96,1,384]{2,1,0:T(2,128)(2,1)S(1)}, bf16[96,1,384]{2,1,0:T(2,128)(2,1)S(1)}, u32[]{:S(2)}, u32[]{:S(2)}) collective-permute-start(bf16[96,1,384]{2,1,0:T(2,128)(2,1)S(1)} %get-tuple-element.3), channel_id=1, source_target_pairs={{1,0},{2,1},{3,2},{4,3},{5,4},{6,5},{7,6},{8,7},{9,8},{10,9},{11,1... | collective-permute-start | bytes 221192 | tf_op jit(solution)/shard_map/ppermute | solution.py:15
  73.1 1.7 %convert_element_type.57 = bf16[96,48,256]{2,1,0:T(8,128)(2,1)} convert(f32[96,48,256]{2,1,0:T(8,128)S(1)} %bitcast.15) | non-fusion elementwise | flops 1179648 | bytes 7077888 | tf_op jit(solution)/shard_map/convert_element_type | solution.py:61
  74.8 1.2 %collective-permute-done = bf16[96,1,384]{2,1,0:T(2,128)(2,1)S(1)} collective-permute-done((bf16[96,1,384]{2,1,0:T(2,128)(2,1)S(1)}, bf16[96,1,384]{2,1,0:T(2,128)(2,1)S(1)}, u32[]{:S(2)}, u32[]{:S(2)}) %collective-permute-start) | collective-permute-done | bytes 73760 | tf_op jit(solution)/shard_map/ppermute | solution.py:14
  75.9 0.0 collective-permute-done.1
  76.0 2.4 %maximum_convert_fusion = f32[96,50,384]{2,1,0:T(8,128)S(1)} fusion(bf16[96,1,384]{2,1,0:T(2,128)(2,1)S(1)} %collective-permute-done.1, bf16[96,48,128]{2,1,0:T(8,128)(2,1)S(1)} %convert.7, bf16[96,48,256]{2,1,0:T(8,128)(2,1)S(1)} %add_convert_fusion, bf16[96,1,384]{2,1,0:T(2,128)(2,1)S(1)} %collective-permute-done), kind=kLoop, calls=%fused_computation.22 | loop fusion | flops 14745600 | bytes 11059200 | tf_op jit(solution)/shard_map/convert_element_type | solution.py:65
  78.4 0.2 slice.49
  78.5 0.0 copy-start.1
  78.6 1.6 %fusion.7 = f32[96,49,256]{2,1,0:T(8,128)S(1)} fusion(f32[96,50,384]{2,1,0:T(8,128)S(1)} %maximum_convert_fusion, f32[96,50,128]{2,1,0:T(8,128)S(1)} %slice.49), kind=kLoop, calls=%fused_computation.12 | loop fusion | flops 7225344 | bytes 16908288 | tf_op jit(solution)/shard_map/add | solution.py:43
  80.1 3.4 %fusion.12 = f32[96,48,256]{2,1,0:T(8,128)} fusion(f32[96,49,256]{2,1,0:T(8,128)S(1)} %fusion.7, f32[96,50,384]{2,1,0:T(8,128)S(1)} %maximum_convert_fusion), kind=kLoop, calls=%fused_computation.19 | loop fusion | flops 2359296 | bytes 18874368 | tf_op jit(solution)/shard_map/sub | solution.py:46
  (7 shorter events, 0.0 us)
Async XLA Ops:
  0.6 2.9 %copy-start = (bf16[256,1024]{1,0:T(8,128)(2,1)S(1)}, bf16[256,1024]{1,0:T(8,128)(2,1)}, u32[]{:S(2)}) copy-start(bf16[256,1024]{1,0:T(8,128)(2,1)} %param.16) | copy-start | bytes 1572868
  0.6 2.7 %copy-start.5 = (f32[96,48]{0,1:T(8,128)S(1)}, f32[96,48]{0,1:T(8,128)}, u32[]{:S(2)}) copy-start(f32[96,48]{0,1:T(8,128)} %param.13) | copy-start | bytes 55300
  0.7 2.9 %copy-start.6 = (bf16[1024]{0:T(1024)(128)(2,1)S(1)}, bf16[1024]{0:T(1024)(128)(2,1)}, u32[]{:S(2)}) copy-start(bf16[1024]{0:T(1024)(128)(2,1)} %param.17) | copy-start | bytes 6148
  24.2 18.5 %copy-start.4 = (s32[96,48]{0,1:T(8,128)S(1)}, s32[96,48]{0,1:T(8,128)}, u32[]{:S(2)}) copy-start(s32[96,48]{0,1:T(8,128)} %param.12) | copy-start | bytes 55300
  24.2 18.7 %copy-start.7 = (bf16[1024,256]{1,0:T(8,128)(2,1)S(1)}, bf16[1024,256]{1,0:T(8,128)(2,1)}, u32[]{:S(2)}) copy-start(bf16[1024,256]{1,0:T(8,128)(2,1)} %param.19) | copy-start | bytes 1572868
  62.3 4.7 %copy-start.3 = (f32[96,48,128]{2,1,0:T(8,128)S(1)}, f32[96,48,128]{2,1,0:T(8,128)}, u32[]{:S(2)}) copy-start(f32[96,48,128]{2,1,0:T(8,128)} %param.11) | copy-start | bytes 7077892
  67.1 6.0 %copy-start.2 = (f32[4608,256]{1,0:T(8,128)S(1)}, f32[4608,256]{1,0:T(8,128)}, u32[]{:S(2)}) copy-start(f32[4608,256]{1,0:T(8,128)} %fusion.3) | copy-start | bytes 14155780
  67.5 8.4 %collective-permute-start = (bf16[96,1,384]{2,1,0:T(2,128)(2,1)S(1)}, bf16[96,1,384]{2,1,0:T(2,128)(2,1)S(1)}, u32[]{:S(2)}, u32[]{:S(2)}) collective-permute-start(bf16[96,1,384]{2,1,0:T(2,128)(2,1)S(1)} %get-tuple-element.2), channel_id=1, source_target_pairs={{0,1},{1,2},{2,3},{3,4},{4,5},{5,6},{6,7},{7,8},{8,9},{9,10},{10,1... | collective-permute-start | bytes 221192 | tf_op jit(solution)/shard_map/ppermute | solution.py:14
  68.0 7.9 %collective-permute-start.1 = (bf16[96,1,384]{2,1,0:T(2,128)(2,1)S(1)}, bf16[96,1,384]{2,1,0:T(2,128)(2,1)S(1)}, u32[]{:S(2)}, u32[]{:S(2)}) collective-permute-start(bf16[96,1,384]{2,1,0:T(2,128)(2,1)S(1)} %get-tuple-element.3), channel_id=1, source_target_pairs={{1,0},{2,1},{3,2},{4,3},{5,4},{6,5},{7,6},{8,7},{9,8},{10,9},{11,1... | collective-permute-start | bytes 221192 | tf_op jit(solution)/shard_map/ppermute | solution.py:15
  78.5 4.9 %copy-start.1 = (bf16[256,1024]{1,0:T(8,128)(2,1)S(1)}, bf16[256,1024]{1,0:T(8,128)(2,1)}, u32[]{:S(2)}) copy-start(bf16[256,1024]{1,0:T(8,128)(2,1)} %param.16) | copy-start | bytes 1572868
where the time goes:
time: 84 us; the launch traced here: 83.5 us
  matrix products  58.5 us (70%)
  other arithmetic  16.8 us (20%)
  starting transfers between devices  5.58 us (7%)
  waiting for transfers between devices  1.19 us (1%)
    dot_general x1, matrix products, short_net(): jnp.dot(hidden, short_mid[0], preferred_element_type=jnp.float32)  20.6 us
    dot_general x1, matrix products, short_net(): jnp.dot(hidden, short_mid[1], preferred_element_type=jnp.float32)  18.5 us
    dot_general x1, matrix products, short_net(): jnp.dot(hidden, short_out, preferred_element_type=jnp.float32)  10.6 us
    dot_general x1, matrix products, long_net(): return jnp.dot(hidden, long_out, preferred_element_type=jnp.float32)  8.84 us
    ppermute x1, starting transfers between devices, padded_2(): after = lax.ppermute(leading, axis, down)  5.07 us
    another operation x2, other arithmetic  4.87 us
    sub x1, other arithmetic, advect(): return padded_state[:, 1:-1] - (east_flux[:, 1:] - east_flux[:, :-1])  3.35 us
    convert_element_type x1, other arithmetic, shards(): columns = state.reshape(column_count, features).astype(jnp.bfloat16)  2.67 us
  transfers between devices with their start and end apart: 2, of which 1 were waited for; matrix products, arithmetic and copies ran while one was open for 2% of the time, Pallas kernels for 0%

commit v1 on v0

v1 whole, which is shorter than its diff:
```python
import functools

import jax
import jax.numpy as jnp
from jax import lax
from jax.experimental import pallas as pl
from jax.experimental.pallas import tpu as pltpu
from jax.sharding import PartitionSpec as P

BF16 = jnp.bfloat16
F32 = jnp.float32


def dot(a, b):
    return jnp.dot(a, b, preferred_element_type=F32)


def silu_of_twice(h):
    return (h + h * jnp.tanh(h)).astype(BF16)


def nets(half_cols, sun_col, w, first_step):
    long_in, long_out, short_in, short_sun, short_mid, short_out, ready = w
    half_sun = sun_col * 0.5
    sun_row = short_sun[...].astype(F32)
    ready(0, first_step)
    first = silu_of_twice(dot(half_cols, short_in[...]) + half_sun * sun_row)
    ready(1, first_step)
    hidden = silu_of_twice(dot(half_cols, long_in[...]))
    ready(2, first_step)
    second = silu_of_twice(dot(first, short_mid[0]) * 0.5)
    ready(3, first_step)
    long_tend = dot(hidden, long_out[...])
    ready(4, first_step)
    third = silu_of_twice(dot(second, short_mid[1]) * 0.5)
    ready(5, first_step)
    short_tend = dot(third, short_out[...])
    return long_tend + jnp.where(sun_col > 0.0, short_tend, 0.0)


def weight_copies(hbm, vmem, sems):
    long_in, long_out, short_in, short_mid, short_out = hbm
    v_long_in, v_long_out, v_short_in, v_short_mid, v_short_out = vmem
    pairs = (
        (short_in, v_short_in),
        (long_in, v_long_in),
        (short_mid.at[0], v_short_mid.at[0]),
        (long_out, v_long_out),
        (short_mid.at[1], v_short_mid.at[1]),
        (short_out, v_short_out),
    )
    return [pltpu.make_async_copy(s, d, sems.at[k]) for k, (s, d) in enumerate(pairs)]


def staged_weights(hbm, vmem, sems, short_sun, first_step):
    copies = weight_copies(hbm, vmem, sems)

    @pl.when(first_step)
    def _():
        for copy in copies:
            copy.start()

    def ready(k, at_first):
        @pl.when(at_first)
        def _():
            copies[k].wait()

    long_in, long_out, short_in, short_mid, short_out = vmem
    return (long_in, long_out, short_in, short_sun, short_mid, short_out, ready)


def lit_sun_column(day_ref, sun_ref, row0, rows):
    lit = jnp.where(day_ref[...] > 0, sun_ref[...], 0.0)
    lane = lax.broadcasted_iota(jnp.int32, lit.shape, 1)
    return jnp.concatenate(
        [
            jnp.sum(jnp.where(lane == row0 + r, lit, 0.0), axis=1, keepdims=True)
            for r in range(rows)
        ],
        axis=0,
    )


def first_kernel(
    rows, day, sun, state, long_in, long_out, short_in, short_sun, short_mid, short_out,
    tend, v0, v1, v2, v3, v4, sems,
):
    i = pl.program_id(0)
    first_step = i == 0
    w = staged_weights(
        (long_in, long_out, short_in, short_mid, short_out), (v0, v1, v2, v3, v4), sems, short_sun, first_step
    )
    _, cells, feats = state.shape[1:]
    cols = rows * cells
    sun_col = lit_sun_column(day, sun, i * rows, rows)
    half_cols = (state[0].reshape(cols, feats) * 0.5).astype(BF16)
    phys = nets(half_cols, sun_col, w, first_step)
    tend[0] = phys.astype(BF16).reshape(rows, cells, feats)


def transport(prov, courant, west_prov, west_cour, east_prov):
    rows, cells, feats = prov.shape
    cols = rows * cells
    pair = jnp.concatenate([courant, courant], axis=-1)
    east_wind, west_wind = jnp.maximum(pair, 0.0), jnp.minimum(pair, 0.0)
    sub = lax.broadcasted_iota(jnp.int32, (rows, 8, feats), 1)
    nxt = pltpu.roll(prov.reshape(cols, feats), cols - 1, 0).reshape(rows, cells, feats)
    tail = jnp.where(sub == 7, east_prov[:, None, :], nxt[:, cells - 8 :])
    nxt = jnp.concatenate([nxt[:, : cells - 8], tail], axis=1)
    flux = east_wind * prov + west_wind * nxt
    prev = pltpu.roll(flux.reshape(cols, feats), 1, 0).reshape(rows, cells, feats)
    wc = jnp.concatenate([west_cour, west_cour], axis=-1)
    face = (jnp.maximum(wc, 0.0) * west_prov)[:, None, :] + jnp.minimum(wc, 0.0)[:, None, :] * prov[:, :8]
    head = jnp.where(sub == 0, face, prev[:, :8])
    prev = jnp.concatenate([head, prev[:, 8:]], axis=1)
    return prov - (flux - prev)


def second_kernel(
    rows, day, sun, state, courant, west_a, west_b, east_a, east_b, tend_in,
    long_in, long_out, short_in, short_sun, short_mid, short_out,
    new_state, tend, v0, v1, v2, v3, v4, sems,
):
    i = pl.program_id(0)
    first_step = i == 0
    w = staged_weights(
        (long_in, long_out, short_in, short_mid, short_out), (v0, v1, v2, v3, v4), sems, short_sun, first_step
    )
    _, cells, feats = state.shape[1:]
    cols = rows * cells
    levels = courant.shape[-1]
    sun_col = lit_sun_column(day, sun, (pl.num_programs(0) + i) * rows, rows)
    halos = (west_a, west_b, east_a, east_b)
    sun_all = jnp.concatenate([sun_col] + [h[:, -1:].astype(F32) for h in halos], axis=0)
    half_cols = jnp.concatenate(
        [(state[1].reshape(cols, feats) * 0.5).astype(BF16)] + [h[:, :feats] * 0.5 for h in halos], axis=0
    )
    phys = nets(half_cols, sun_all, w, first_step)
    own = phys[:cols].reshape(rows, cells, feats)
    tend[0] = own.astype(BF16)
    edge = [
        h[:, :feats].astype(F32) + phys[cols + k * rows : cols + (k + 1) * rows] for k, h in enumerate(halos)
    ]
    new_state[0] = transport(
        state[0] + tend_in[0].astype(F32), courant[0],
        edge[0], west_a[:, feats : feats + levels].astype(F32), edge[2],
    )
    new_state[1] = transport(
        state[1] + own, courant[1],
        edge[1], west_b[:, feats : feats + levels].astype(F32), edge[3],
    )


def shards(
    state, courant, daylit, insolation, long_in, long_out, short_in, short_sun, short_mid, short_out
):
    lat_rows, cells, feats = state.shape
    levels = courant.shape[-1]
    hid = long_in.shape[1]
    size = lax.axis_size("lon")
    up = [(i, (i + 1) % size) for i in range(size)]
    down = [(j, i) for i, j in up]

    def packed(at, with_courant):
        lit = jnp.where(daylit[:, at] > 0, insolation[:, at], 0.0)
        parts = [state[:, at]] + ([courant[:, at]] if with_courant else [])
        parts.append(jnp.broadcast_to(lit[:, None], (lat_rows, 128)))
        return jnp.concatenate(parts, axis=-1).astype(BF16)

    west = lax.ppermute(packed(cells - 1, True), "lon", up)
    east = lax.ppermute(packed(0, False), "lon", down)

    half = lat_rows // 2
    rows = 16
    steps = half // rows
    day_t, sun_t = daylit.T, insolation.T
    state4 = state.reshape(2, half, cells, feats)
    courant4 = courant.reshape(2, half, cells, levels)
    sun_row = short_sun.reshape(1, hid)
    weights = (long_in, long_out, short_in, sun_row, short_mid, short_out)
    any_spec = pl.BlockSpec(memory_space=pl.ANY)
    small = pl.BlockSpec((cells, lat_rows), lambda i: (0, 0))
    weight_specs = [any_spec, any_spec, any_spec, pl.BlockSpec((1, hid), lambda i: (0, 0)), any_spec, any_spec]
    scratch = [
        pltpu.VMEM((feats, hid), BF16),
        pltpu.VMEM((hid, feats), BF16),
        pltpu.VMEM((feats, hid), BF16),
        pltpu.VMEM((2, hid, hid), BF16),
        pltpu.VMEM((hid, feats), BF16),
        pltpu.SemaphoreType.DMA((6,)),
    ]
    macs = 4 * feats * hid + 2 * hid * hid

    def grid_block(lead, last, at):
        return pl.BlockSpec((lead, rows, cells, last), lambda i: (at, i, 0, 0))

    params = pltpu.CompilerParams(vmem_limit_bytes=48 * 2**20)
    tend_shape = jax.ShapeDtypeStruct((2, half, cells, feats), BF16)
    tend = pl.pallas_call(
        functools.partial(first_kernel, rows),
        grid=(steps,),
        in_specs=[small, small, grid_block(1, feats, 0)] + weight_specs,
        out_specs=grid_block(1, feats, 0),
        out_shape=tend_shape,
        scratch_shapes=scratch,
        compiler_params=params,
        cost_estimate=pl.CostEstimate(
            flops=2 * half * cells * macs, bytes_accessed=10 * 2**20, transcendentals=0
        ),
        name="nets_first_half",
    )(day_t, sun_t, state4, *weights)

    def halo_spec(last, offset):
        return pl.BlockSpec((rows, last), lambda i: (i + offset, 0))

    new_state, tend = pl.pallas_call(
        functools.partial(second_kernel, rows),
        grid=(steps,),
        in_specs=[
            small, small, grid_block(2, feats, 0), grid_block(2, levels, 0),
            halo_spec(feats + levels + 128, 0), halo_spec(feats + levels + 128, steps),
            halo_spec(feats + 128, 0), halo_spec(feats + 128, steps),
            grid_block(1, feats, 0),
        ] + weight_specs,
        out_specs=(grid_block(2, feats, 0), grid_block(1, feats, 1)),
        out_shape=(jax.ShapeDtypeStruct((2, half, cells, feats), F32), tend_shape),
        input_output_aliases={8: 1},
        scratch_shapes=scratch,
        compiler_params=params,
        cost_estimate=pl.CostEstimate(
            flops=2 * half * (cells + 4) * macs, bytes_accessed=24 * 2**20, transcendentals=0
        ),
        name="nets_second_half_transport",
    )(day_t, sun_t, state4, courant4, west, west, east, east, tend, *weights)
    return new_state.reshape(state.shape), tend.reshape(state.shape)


def solution(mesh):
    in_specs = (
        P("ens", "lon", None),
        P("ens", "lon", None),
        P("ens", "lon"),
        P("ens", "lon"),
        P(),
        P(),
        P(),
        P(),
        P(),
        P(),
    )
    out_specs = (P("ens", "lon", None), P("ens", "lon", None))
    return jax.shard_map(shards, mesh=mesh, in_specs=in_specs, out_specs=out_specs, check_vma=False)
```

time: 84 us -> 60.6 us (0.72)
  matrix products: 58.5 us -> 0 us
  Pallas kernels: 0 us -> 48.7 us
  other arithmetic: 16.8 us -> 0.03 us
  local copies, waits for them, and re-layouts: 0.57 us -> 5.25 us
  waiting for transfers between devices: 1.19 us -> 0.01 us
    dot_general x4 -> x0, matrix products: 58.5 us -> none  [the longest x1 20.6 us: short_net(): jnp.dot(hidden, short_mid[0], preferred_element_type=jnp.float32)]
    pallas_call x0 -> x2, Pallas kernels: none -> 48.7 us  [the longest x1 26.9 us: shards(): pl.pallas_call(functools.partial(second_kernel, rows), grid=(steps,), in_...]
    convert_element_type x5 -> x0, other arithmetic: 6.75 us -> none  [the longest x1 2.67 us: shards(): columns = state.reshape(column_count, features).astype(jnp.bfloat16)]
    unnamed x17 -> x18, local copies, waits for them, and re-layouts: 0.13 us -> 5.04 us
    another operation x2 -> x1, other arithmetic: 4.87 us -> 0.01 us
    sub x1 -> x0, other arithmetic: 3.35 us -> none  [advect(): return padded_state[:, 1:-1] - (east_flux[:, 1:] - east_flux[:, :-1])]
    add x1 -> x0, other arithmetic: 1.57 us -> none  [advect(): jnp.maximum(courant_pair, 0.0) * padded_state[:, :-1]]
    ppermute x2, waiting for transfers between devices: 1.19 us -> 0.01 us  [the longest x1 0.01 us: shards(): west = lax.ppermute(packed(cells - 1, True), 'lon', up)]
  transfers between devices with their start and end apart: 2 -> 2, of which waited for: 1 -> 0; matrix products, arithmetic and copies ran while one was open for 2% -> 0% of each run, Pallas kernels for 0% -> 36%
where the time goes in v1:
time: 60.6 us; the launch traced here: 60.5 us
  Pallas kernels  48.7 us (80%)
  starting transfers between devices  5.55 us (9%)
  local copies, waits for them, and re-layouts  5.25 us (9%)
  between operations  1 us (2%)
    pallas_call x1, Pallas kernels, shards(): pl.pallas_call(functools.partial(second_kernel, rows), grid=(steps,), in_...  26.9 us
    pallas_call x1, Pallas kernels, shards(): pl.pallas_call(functools.partial(first_kernel, rows), grid=(steps,), in_s...  21.7 us
    ppermute x1, starting transfers between devices, shards(): east = lax.ppermute(packed(0, False), 'lon', down)  5.5 us
    unnamed x18, local copies, waits for them, and re-layouts  5.04 us
  transfers between devices with their start and end apart: 2, of which 0 were waited for; matrix products, arithmetic and copies ran while one was open for 0% of the time, Pallas kernels for 36%

profile of v1, /device:TPU:0, one launch (start us, length us, event | category | flops | bytes accessed | tf_op | source)
XLA Modules:
  0.0 60.5 jit_solution(5491462391170675224)
XLA Ops:
  0.6 0.0 copy-start.2
  0.6 0.0 copy-start.1
  0.7 0.0 copy-start
  0.7 0.0 copy-start.7
  0.7 0.0 copy-start.6
  0.7 0.0 copy-start.5
  0.7 0.0 copy-start.4
  0.7 0.0 copy-start.3
  0.7 5.0 %copy.20 = bf16[96,48,256]{2,0,1:T(8,128)(2,1)S(1)} copy(f32[96,48,256]{2,1,0:T(8,128)} %param.10) | data formatting | bytes 7077888 | tf_op args[0]
  5.7 0.0 copy-done.2
  5.7 0.0 copy-done.1
  5.8 0.1 broadcast_in_dim.25
  5.9 5.5 %collective-permute-start.1 = (bf16[96,384]{1,0:T(8,128)(2,1)S(1)}, bf16[96,384]{1,0:T(8,128)(2,1)S(1)}, u32[]{:S(2)}, u32[]{:S(2)}) collective-permute-start(bf16[96,384]{1,0:T(8,128)(2,1)S(1)} %pad_maximum_fusion.1), channel_id=1, source_target_pairs={{1,0},{2,1},{3,2},{4,3},{5,4},{6,5},{7,6},{8,7},{9,8},{10,9},{11,1... | collective-permute-start | bytes 221192 | tf_op jit(solution)/shard_map/ppermute | solution.py:171
  11.4 0.0 copy-done
  11.4 0.1 broadcast_in_dim.23
  11.5 0.1 collective-permute-start
  11.6 0.0 copy-done.7
  11.6 0.0 copy-done.6
  11.6 0.0 copy-done.5
  11.6 0.0 copy-done.4
  11.6 0.0 copy-done.3
  11.6 21.7 %nets_first_half.1.tend_in = bf16[2,48,48,256]{3,2,1,0:T(8,128)(2,1)} custom-call(s32[48,96]{1,0:T(8,128)S(1)} %bitcast.18, f32[48,96]{1,0:T(8,128)S(1)} %bitcast.20, f32[2,48,48,256]{3,2,1,0:T(8,128)} %bitcast.22, bf16[256,1024]{1,0:T(8,128)(2,1)S(1)} %copy-done.3, bf16[1024,256]{1,0:T(8,128)(2,1)S(1)} %copy-done.4, bf16[256,1024]{1,0:T(8,128)(2,1)S(1)} %copy-done.5, ...), custom_call_target="tpu_custom_call" | custom-call | flops 14495514624 | bytes 10485760 | tf_op jit(solution)/shard_map/nets_first_half/pallas_call | solution.py:199
  33.4 0.0 collective-permute-done.1.east_a.east_b
  33.4 0.0 collective-permute-done.west_a.west_b
  33.4 26.9 %nets_second_half_transport.1 = (f32[2,48,48,256]{3,2,1,0:T(8,128)}, bf16[2,48,48,256]{3,2,1,0:T(8,128)(2,1)}) custom-call(s32[48,96]{1,0:T(8,128)S(1)} %bitcast.19, f32[48,96]{1,0:T(8,128)S(1)} %bitcast.21, f32[2,48,48,256]{3,2,1,0:T(8,128)} %bitcast.23, f32[2,48,48,128]{3,2,1,0:T(8,128)S(1)} %bitcast.17, ...), custom_call_target="tpu_custom_call", output_to_operand_aliasing={{1}: (8, {})} | custom-call | flops 15703474176 | bytes 25165824 | tf_op jit(solution)/shard_map/nets_second_half_transport/pallas_call | solution.py:216
  (7 shorter events, 0.1 us)
Async XLA Ops:
  0.6 5.1 %copy-start.2 = (f32[96,48]{0,1:T(8,128)S(1)}, f32[96,48]{0,1:T(8,128)}, u32[]{:S(2)}) copy-start(f32[96,48]{0,1:T(8,128)} %param.13) | copy-start | bytes 55300
  0.6 5.1 %copy-start.1 = (s32[96,48]{0,1:T(8,128)S(1)}, s32[96,48]{0,1:T(8,128)}, u32[]{:S(2)}) copy-start(s32[96,48]{0,1:T(8,128)} %param.12) | copy-start | bytes 55300
  0.7 10.7 %copy-start = (f32[96,48,128]{2,1,0:T(8,128)S(1)}, f32[96,48,128]{2,1,0:T(8,128)}, u32[]{:S(2)}) copy-start(f32[96,48,128]{2,1,0:T(8,128)} %param.11) | copy-start | bytes 7077892
  0.7 10.9 %copy-start.7 = (bf16[1024]{0:T(1024)(128)(2,1)S(1)}, bf16[1024]{0:T(1024)(128)(2,1)}, u32[]{:S(2)}) copy-start(bf16[1024]{0:T(1024)(128)(2,1)} %param.17) | copy-start | bytes 6148
  0.7 10.9 %copy-start.6 = (bf16[1024,256]{1,0:T(8,128)(2,1)S(1)}, bf16[1024,256]{1,0:T(8,128)(2,1)}, u32[]{:S(2)}) copy-start(bf16[1024,256]{1,0:T(8,128)(2,1)} %short_out.3) | copy-start | bytes 1572868
  0.7 10.9 %copy-start.5 = (bf16[256,1024]{1,0:T(8,128)(2,1)S(1)}, bf16[256,1024]{1,0:T(8,128)(2,1)}, u32[]{:S(2)}) copy-start(bf16[256,1024]{1,0:T(8,128)(2,1)} %short_in.3) | copy-start | bytes 1572868
  0.7 10.9 %copy-start.4 = (bf16[1024,256]{1,0:T(8,128)(2,1)S(1)}, bf16[1024,256]{1,0:T(8,128)(2,1)}, u32[]{:S(2)}) copy-start(bf16[1024,256]{1,0:T(8,128)(2,1)} %long_out.3) | copy-start | bytes 1572868
  0.7 10.9 %copy-start.3 = (bf16[256,1024]{1,0:T(8,128)(2,1)S(1)}, bf16[256,1024]{1,0:T(8,128)(2,1)}, u32[]{:S(2)}) copy-start(bf16[256,1024]{1,0:T(8,128)(2,1)} %long_in.3) | copy-start | bytes 1572868
  5.9 27.5 %collective-permute-start.1 = (bf16[96,384]{1,0:T(8,128)(2,1)S(1)}, bf16[96,384]{1,0:T(8,128)(2,1)S(1)}, u32[]{:S(2)}, u32[]{:S(2)}) collective-permute-start(bf16[96,384]{1,0:T(8,128)(2,1)S(1)} %pad_maximum_fusion.1), channel_id=1, source_target_pairs={{1,0},{2,1},{3,2},{4,3},{5,4},{6,5},{7,6},{8,7},{9,8},{10,9},{11,1... | collective-permute-start | bytes 221192 | tf_op jit(solution)/shard_map/ppermute | solution.py:171
  11.5 21.9 %collective-permute-start = (bf16[96,512]{1,0:T(8,128)(2,1)S(1)}, bf16[96,512]{1,0:T(8,128)(2,1)S(1)}, u32[]{:S(2)}, u32[]{:S(2)}) collective-permute-start(bf16[96,512]{1,0:T(8,128)(2,1)S(1)} %pad_maximum_fusion), channel_id=1, source_target_pairs={{0,1},{1,2},{2,3},{3,4},{4,5},{5,6},{6,7},{7,8},{8,9},{9,10},{10,1... | collective-permute-start | bytes 294920 | tf_op jit(solution)/shard_map/ppermute | solution.py:170

commit v2 on v1

v2 whole, which is shorter than its diff:
```python
import functools

import jax
import jax.numpy as jnp
from jax import lax
from jax.experimental import pallas as pl
from jax.experimental.pallas import tpu as pltpu
from jax.sharding import PartitionSpec as P

BF16 = jnp.bfloat16
F32 = jnp.float32


def dot(a, b):
    return jnp.dot(a, b, preferred_element_type=F32)


def silu_of_twice(h):
    return (h + h * jnp.tanh(h)).astype(BF16)


def nets(half_cols, sun_col, w):
    long_in, long_out, short_in, short_sun, short_mid, short_out = w
    half_sun = sun_col * 0.5
    sun_row = short_sun[...].astype(F32)
    first = silu_of_twice(dot(half_cols, short_in[...]) + half_sun * sun_row)
    hidden = silu_of_twice(dot(half_cols, long_in[...]))
    second = silu_of_twice(dot(first, short_mid[0]) * 0.5)
    long_tend = dot(hidden, long_out[...])
    third = silu_of_twice(dot(second, short_mid[1]) * 0.5)
    short_tend = dot(third, short_out[...])
    return long_tend + jnp.where(sun_col > 0.0, short_tend, 0.0)


def lit_sun_column(day_ref, sun_ref, row0, rows):
    lit = jnp.where(day_ref[...] > 0, sun_ref[...], 0.0)
    lane = lax.broadcasted_iota(jnp.int32, lit.shape, 1)
    return jnp.concatenate(
        [
            jnp.sum(jnp.where(lane == row0 + r, lit, 0.0), axis=1, keepdims=True)
            for r in range(rows)
        ],
        axis=0,
    )


def pack_kernel(day, sun, state_w, state_e, courant_w, courant_e, out_a, out_b):
    feats, levels = state_w.shape[-1], courant_w.shape[-1]
    end = feats + levels
    cells, lat_rows = day.shape
    odd = lax.rem(lax.axis_index("lon"), 2) == 1
    lit = jnp.where(day[...] > 0, sun[...], 0.0)

    def choose(east, west):
        return jnp.where(odd, west, east).astype(BF16), jnp.where(odd, east, west).astype(BF16)

    for lanes, (a, b) in (
        (slice(0, feats), choose(state_e[:, 7, :], state_w[:, 0, :])),
        (slice(feats, end), choose(courant_e[:, 7, :], courant_w[:, 0, :])),
    ):
        out_a[:, lanes] = a
        out_b[:, lanes] = b
    for out, row in zip((out_a, out_b), choose(lit[cells - 1 :], lit[:1])):
        out[:, end:] = jnp.zeros((lat_rows, out.shape[1] - end), BF16)
        out[:16, end : end + lat_rows] = jnp.broadcast_to(row, (16, lat_rows))


def first_kernel(rows, day, sun, state, *rest):
    *w, tend = rest
    i = pl.program_id(0)
    _, _, cells, feats = state.shape
    cols = rows * cells
    sun_col = lit_sun_column(day, sun, i * rows, rows)
    half_cols = (state[0].reshape(cols, feats) * 0.5).astype(BF16)
    tend[0] = nets(half_cols, sun_col, w).astype(BF16).reshape(rows, cells, feats)


def transport(prov, courant, west_prov, west_cour, east_prov):
    rows, cells, feats = prov.shape
    cols = rows * cells
    pair = jnp.concatenate([courant, courant], axis=-1)
    east_wind, west_wind = jnp.maximum(pair, 0.0), jnp.minimum(pair, 0.0)
    sub = lax.broadcasted_iota(jnp.int32, (rows, 8, feats), 1)
    nxt = pltpu.roll(prov.reshape(cols, feats), cols - 1, 0).reshape(rows, cells, feats)
    tail = jnp.where(sub == 7, east_prov[:, None, :], nxt[:, cells - 8 :])
    nxt = jnp.concatenate([nxt[:, : cells - 8], tail], axis=1)
    flux = east_wind * prov + west_wind * nxt
    prev = pltpu.roll(flux.reshape(cols, feats), 1, 0).reshape(rows, cells, feats)
    wc = jnp.concatenate([west_cour, west_cour], axis=-1)
    face = (jnp.maximum(wc, 0.0) * west_prov)[:, None, :] + jnp.minimum(wc, 0.0)[:, None, :] * prov[:, :8]
    head = jnp.where(sub == 0, face, prev[:, :8])
    prev = jnp.concatenate([head, prev[:, 8:]], axis=1)
    return prov - (flux - prev)


def second_kernel(
    rows, day, sun, state, state_lo, courant, a_lo, a_hi, a_sun, b_lo, b_hi, b_sun, tend_lo,
    long_in, long_out, short_in, short_sun, short_mid, short_out,
    new_state, tend, prov, edges, west_wind,
):
    i = pl.program_id(0)
    tiles = pl.num_programs(0) - 1
    _, _, cells, feats = state.shape
    cols = rows * cells
    levels = courant.shape[-1]
    odd = lax.rem(lax.axis_index("lon"), 2) == 1

    def column_nets():
        row0 = (tiles + i) * rows
        sun_col = lit_sun_column(day, sun, row0, rows)
        west_lo = jnp.where(odd, a_lo[0].astype(F32), b_lo[0].astype(F32))
        west_hi = jnp.where(odd, a_hi[0].astype(F32), b_hi[0].astype(F32))
        east_lo = jnp.where(odd, b_lo[1].astype(F32), a_lo[1].astype(F32))
        east_hi = jnp.where(odd, b_hi[1].astype(F32), a_hi[1].astype(F32))
        halos = [h[:, :feats] for h in (west_lo, west_hi, east_lo, east_hi)]
        lat_rows = day.shape[1]
        west_sun = jnp.where(odd, a_sun[0].astype(F32), b_sun[0].astype(F32))
        east_sun = jnp.where(odd, b_sun[1].astype(F32), a_sun[1].astype(F32))
        lane = lax.broadcasted_iota(jnp.int32, west_sun.shape, 1)
        sub = lax.broadcasted_iota(jnp.int32, west_sun.shape, 0)
        suns = [
            jnp.sum(jnp.where(lane == sub + at, lit, 0.0), axis=1, keepdims=True)
            for lit, at in ((west_sun, i * rows), (west_sun, row0), (east_sun, i * rows), (east_sun, row0))
        ]
        sun_all = jnp.concatenate([sun_col] + suns, axis=0)
        own_state = state[0].reshape(cols, feats)
        half_cols = (jnp.concatenate([own_state] + halos, axis=0) * 0.5).astype(BF16)
        phys = nets(half_cols, sun_all, (long_in, long_out, short_in, short_sun, short_mid, short_out))
        tend[0] = phys[:cols].astype(BF16).reshape(rows, cells, feats)
        prov[...] = (own_state + phys[:cols]).reshape(rows, cells, feats)
        edges[...] = jnp.concatenate(halos, axis=0) + phys[cols:]
        west_wind[...] = jnp.concatenate([west_lo, west_hi], axis=0)[:, feats : feats + levels]

    def move():
        new_state[0] = transport(
            state_lo[0] + tend_lo[0].astype(F32), courant[0],
            edges[:rows], west_wind[:rows], edges[2 * rows : 3 * rows],
        )
        new_state[1] = transport(
            prov[...], courant[1], edges[rows : 2 * rows], west_wind[rows:], edges[3 * rows :],
        )

    @pl.when(i == 0)
    def _():
        column_nets()

    @pl.when(jnp.logical_and(i > 0, i < tiles))
    def _():
        move()
        column_nets()

    @pl.when(i == tiles)
    def _():
        move()


def exchange(edge_a, edge_b, pairs, seams):
    return (
        lax.all_gather(edge_a, "lon", axis_index_groups=pairs),
        lax.all_gather(edge_b, "lon", axis_index_groups=seams),
    )


def shards(
    state, courant, daylit, insolation, long_in, long_out, short_in, short_sun, short_mid, short_out
):
    lat_rows, cells, feats = state.shape
    levels = courant.shape[-1]
    hid = long_in.shape[1]
    size = lax.axis_size("lon")
    rows = 16
    half = lat_rows // 2
    steps = half // rows
    width = feats + levels + 128
    day_t, sun_t = daylit.T, insolation.T
    small = pl.BlockSpec((cells, lat_rows), lambda *i: (0, 0))
    last = cells // 8 - 1

    def edge_block(depth, at):
        return pl.BlockSpec((lat_rows, 8, depth), lambda i: (0, at, 0))

    edge_shape = jax.ShapeDtypeStruct((lat_rows, width), BF16)
    edge_out = pl.BlockSpec((lat_rows, width), lambda i: (0, 0))
    edge_a, edge_b = pl.pallas_call(
        pack_kernel,
        grid=(1,),
        in_specs=[small, small, edge_block(feats, 0), edge_block(feats, last), edge_block(levels, 0), edge_block(levels, last)],
        out_specs=(edge_out, edge_out),
        out_shape=(edge_shape, edge_shape),
        cost_estimate=pl.CostEstimate(flops=0, bytes_accessed=3 * 2**20, transcendentals=0),
        name="edges_packed",
    )(day_t, sun_t, state, state, courant, courant)
    pairs = [[i, i + 1] for i in range(0, size, 2)]
    seams = [[i, (i + 1) % size] for i in range(1, size, 2)]
    halo_a, halo_b = exchange(edge_a, edge_b, pairs, seams)

    state4 = state.reshape(2, half, cells, feats)
    courant4 = courant.reshape(2, half, cells, levels)
    weights = tuple(
        pltpu.with_memory_space_constraint(w, pltpu.VMEM)
        for w in (long_in, long_out, short_in, short_sun.reshape(1, hid), short_mid, short_out)
    )
    weight_specs = [pl.BlockSpec(memory_space=pltpu.VMEM)] * 6
    macs = 4 * feats * hid + 2 * hid * hid
    params = pltpu.CompilerParams(vmem_limit_bytes=44 * 2**20)
    tend_shape = jax.ShapeDtypeStruct((2, half, cells, feats), BF16)
    tend = pl.pallas_call(
        functools.partial(first_kernel, rows),
        grid=(steps,),
        in_specs=[small, small, pl.BlockSpec((1, rows, cells, feats), lambda i: (0, i, 0, 0))] + weight_specs,
        out_specs=pl.BlockSpec((1, rows, cells, feats), lambda i: (0, i, 0, 0)),
        out_shape=tend_shape,
        compiler_params=params,
        cost_estimate=pl.CostEstimate(
            flops=2 * half * cells * macs, bytes_accessed=10 * 2**20, transcendentals=0
        ),
        name="nets_first_half",
    )(day_t, sun_t, state4, *weights)

    def here(i):
        return jnp.minimum(i, steps - 1)

    def before(i):
        return jnp.maximum(i - 1, 0)

    def block(lead, depth, at, when):
        return pl.BlockSpec((lead, rows, cells, depth), lambda i: (at, when(i), 0, 0))

    halo_lo = pl.BlockSpec((2, rows, width), lambda i: (0, here(i), 0))
    halo_hi = pl.BlockSpec((2, rows, width), lambda i: (0, steps + here(i), 0))
    halo_sun = pl.BlockSpec((2, 16, 128), lambda i: (0, 0, width // 128 - 1))
    new_state, tend = pl.pallas_call(
        functools.partial(second_kernel, rows),
        grid=(steps + 1,),
        in_specs=[
            small, small, block(1, feats, 1, here), block(1, feats, 0, before), block(2, levels, 0, before),
            halo_lo, halo_hi, halo_sun, halo_lo, halo_hi, halo_sun,
            block(1, feats, 0, before),
        ] + weight_specs,
        out_specs=(block(2, feats, 0, before), block(1, feats, 1, here)),
        out_shape=(jax.ShapeDtypeStruct((2, half, cells, feats), F32), tend_shape),
        input_output_aliases={11: 1},
        scratch_shapes=[
            pltpu.VMEM((rows, cells, feats), F32),
            pltpu.VMEM((4 * rows, feats), F32),
            pltpu.VMEM((2 * rows, levels), F32),
        ],
        compiler_params=params,
        cost_estimate=pl.CostEstimate(
            flops=2 * half * (cells + 4) * macs, bytes_accessed=24 * 2**20, transcendentals=0
        ),
        name="nets_second_half_transport",
    )(day_t, sun_t, state4, state4, courant4, halo_a, halo_a, halo_a, halo_b, halo_b, halo_b, tend, *weights)
    return new_state.reshape(state.shape), tend.reshape(state.shape)


def solution(mesh):
    in_specs = (
        P("ens", "lon", None),
        P("ens", "lon", None),
        P("ens", "lon"),
        P("ens", "lon"),
        P(),
        P(),
        P(),
        P(),
        P(),
        P(),
    )
    out_specs = (P("ens", "lon", None), P("ens", "lon", None))
    return jax.shard_map(shards, mesh=mesh, in_specs=in_specs, out_specs=out_specs, check_vma=False)
```

time: 60.6 us -> 58.5 us (0.965)
  blocking collectives: 0 us -> 11.1 us
  starting transfers between devices: 5.55 us -> 0 us
  Pallas kernels: 48.7 us -> 43.5 us
  local copies, waits for them, and re-layouts: 5.25 us -> 2.91 us
    all_gather x0 -> x2, blocking collectives: none -> 11.1 us  [the longest x1 8.89 us: exchange(): lax.all_gather(edge_b, 'lon', axis_index_groups=seams)]
    ppermute x2 -> x0, starting transfers between devices: 5.55 us -> none  [the longest x1 5.5 us: shards(): east = lax.ppermute(packed(0, False), 'lon', down)]
    pallas_call x1, Pallas kernels: 21.7 us -> 17.8 us  [shards(): pl.pallas_call(functools.partial(first_kernel, rows), grid=(steps,), in_s...]
    unnamed x18, local copies, waits for them, and re-layouts: 5.04 us -> 2.22 us
    pallas_call x1 -> x2, Pallas kernels: 26.9 us -> 25.7 us  [the longest x1 22.9 us: shards(): pl.pallas_call(functools.partial(second_kernel, rows), grid=(steps + 1,),...]
    reshape x1, local copies, waits for them, and re-layouts: 0.01 us -> 0.69 us  [shards(): short_sun.reshape(1, hid)]
  transfers between devices with their start and end apart: 2 -> 0, of which waited for: 0 -> 0; matrix products, arithmetic and copies ran while one was open for 0% -> 0% of each run, Pallas kernels for 36% -> 0%
where the time goes in v2:
time: 58.5 us; the launch traced here: 58.2 us
  Pallas kernels  43.5 us (74%)
  blocking collectives  11.1 us (19%)
  local copies, waits for them, and re-layouts  2.91 us (5%)
  between operations  0.7 us (1%)
    pallas_call x1, Pallas kernels, shards(): pl.pallas_call(functools.partial(second_kernel, rows), grid=(steps + 1,),...  22.9 us
    pallas_call x1, Pallas kernels, shards(): pl.pallas_call(functools.partial(first_kernel, rows), grid=(steps,), in_s...  17.8 us
    all_gather x1, blocking collectives, exchange(): lax.all_gather(edge_b, 'lon', axis_index_groups=seams)  8.89 us
    pallas_call x1, Pallas kernels, shards(): pl.pallas_call(pack_kernel, grid=(1,), in_specs=[small, small, edge_block...  2.88 us
    all_gather x1, blocking collectives, exchange(): lax.all_gather(edge_a, 'lon', axis_index_groups=pairs)  2.24 us
    unnamed x18, local copies, waits for them, and re-layouts  2.22 us

profile of v2, /device:TPU:0, one launch (start us, length us, event | category | flops | bytes accessed | tf_op | source)
XLA Modules:
  0.0 58.2 jit_solution(5658426652345620550)
XLA Ops:
  0.6 0.7 %reshape.21.rest_3_.short_sun = bf16[1,1024]{1,0:T(2,128)(2,1)S(1)} reshape(bf16[1024]{0:T(1024)(128)(2,1)} %param.17) | data formatting | bytes 4096 | tf_op jit(solution)/shard_map/reshape | solution.py:201
  1.3 0.0 copy-start.1
  1.3 0.0 copy-start.2
  1.3 0.0 copy-start.5
  1.3 0.0 copy-start.6
  1.3 0.0 copy-start.7
  1.4 0.0 copy-start.8
  1.4 2.9 %edges_packed.1 = (bf16[96,512]{1,0:T(8,128)(2,1)}, bf16[96,512]{1,0:T(8,128)(2,1)}) custom-call(s32[48,96]{1,0:T(8,128)} %bitcast.15, f32[48,96]{1,0:T(8,128)} %bitcast.18, f32[96,48,256]{2,1,0:T(8,128)} %state_e.1, f32[96,48,256]{2,1,0:T(8,128)} %state_e.1, f32[96,48,128]{2,1,0:T(8,128)} %courant_e.1, f32[96,48,128]{2,1,0:T(8,128)} %courant_e.1), custom_call_target="tpu_custom_call" | custom-call | bytes 3145728 | tf_op jit(solution)/shard_map/edges_packed/pallas_call | solution.py:184
  4.2 2.2 %all-gather = bf16[192,512]{1,0:T(8,128)(2,1)S(1)} all-gather(bf16[96,512]{1,0:T(8,128)(2,1)} %get-tuple-element.6), channel_id=2, replica_groups={{0,1},{2,3},{4,5},{6,7},{8,9},{10,11},{12,13},{14,15},{16,17},{18,19},{..., dimensions={0}, use_global_device_ids=true | all-gather | bytes 294912 | tf_op jit(solution)/shard_map/all_gather | solution.py:159
  6.5 8.9 %all-gather.1 = bf16[192,512]{1,0:T(8,128)(2,1)S(1)} all-gather(bf16[96,512]{1,0:T(8,128)(2,1)} %get-tuple-element.7), channel_id=3, replica_groups={{1,2},{3,4},{5,6},{7,8},{9,10},{11,12},{13,14},{15,0},{17,18},{19,20},{..., dimensions={0}, use_global_device_ids=true | all-gather | bytes 294912 | tf_op jit(solution)/shard_map/all_gather | solution.py:160
  15.4 0.0 copy-done.1
  15.4 0.0 copy-done.2
  15.4 0.0 copy-done.5
  15.4 0.0 copy-done.6
  15.4 0.0 copy-done.7
  15.4 0.0 copy-done.8
  15.4 0.0 copy-start.3
  15.4 2.2 %copy-done.3 = bf16[2,1024,1024]{2,1,0:T(8,128)(2,1)S(1)} copy-done((bf16[2,1024,1024]{2,1,0:T(8,128)(2,1)S(1)}, bf16[2,1024,1024]{2,1,0:T(8,128)(2,1)}, u32[]{:S(2)}) %copy-start.3) | copy-done | bytes 4194328
  17.6 0.0 copy-start
  17.6 0.0 copy-start.4
  17.6 17.8 %nets_first_half.1.tend_lo = bf16[2,48,48,256]{3,2,1,0:T(8,128)(2,1)} custom-call(s32[48,96]{1,0:T(8,128)S(1)} %bitcast.16, f32[48,96]{1,0:T(8,128)S(1)} %bitcast.19, f32[2,48,48,256]{3,2,1,0:T(8,128)} %bitcast.21, bf16[256,1024]{1,0:T(8,128)(2,1)S(1)} %copy-done.5, bf16[1024,256]{1,0:T(8,128)(2,1)S(1)} %copy-done.6, bf16[256,1024]{1,0:T(8,128)(2,1)S(1)} %copy-done.7, ...), custom_call_target="tpu_custom_call" | custom-call | flops 14495514624 | bytes 10485760 | tf_op jit(solution)/shard_map/nets_first_half/pallas_call | solution.py:207
  35.4 0.0 copy-done
  35.4 0.0 copy-done.4
  35.4 22.9 %nets_second_half_transport.1 = (f32[2,48,48,256]{3,2,1,0:T(8,128)}, bf16[2,48,48,256]{3,2,1,0:T(8,128)(2,1)}) custom-call(s32[48,96]{1,0:T(8,128)S(1)} %bitcast.17, f32[48,96]{1,0:T(8,128)S(1)} %bitcast.20, f32[2,48,48,256]{3,2,1,0:T(8,128)} %bitcast.22, f32[2,48,48,256]{3,2,1,0:T(8,128)} %bitcast.23, ...), custom_call_target="tpu_custom_call", output_to_operand_aliasing={{1}: (11, {})} | custom-call | flops 15703474176 | bytes 25165824 | tf_op jit(solution)/shard_map/nets_second_half_transport/pallas_call | solution.py:232
Async XLA Ops:
  1.3 14.1 %copy-start.1 = (s32[96,48]{0,1:T(8,128)S(1)}, s32[96,48]{0,1:T(8,128)}, u32[]{:S(2)}) copy-start(s32[96,48]{0,1:T(8,128)} %param.12) | copy-start | bytes 55300
  1.3 14.1 %copy-start.2 = (f32[96,48]{0,1:T(8,128)S(1)}, f32[96,48]{0,1:T(8,128)}, u32[]{:S(2)}) copy-start(f32[96,48]{0,1:T(8,128)} %param.13) | copy-start | bytes 55300
  1.3 14.1 %copy-start.5 = (bf16[256,1024]{1,0:T(8,128)(2,1)S(1)}, bf16[256,1024]{1,0:T(8,128)(2,1)}, u32[]{:S(2)}) copy-start(bf16[256,1024]{1,0:T(8,128)(2,1)} %long_in.1) | copy-start | bytes 1572868
  1.3 14.1 %copy-start.6 = (bf16[1024,256]{1,0:T(8,128)(2,1)S(1)}, bf16[1024,256]{1,0:T(8,128)(2,1)}, u32[]{:S(2)}) copy-start(bf16[1024,256]{1,0:T(8,128)(2,1)} %long_out.1) | copy-start | bytes 1572868
  1.3 14.1 %copy-start.7 = (bf16[256,1024]{1,0:T(8,128)(2,1)S(1)}, bf16[256,1024]{1,0:T(8,128)(2,1)}, u32[]{:S(2)}) copy-start(bf16[256,1024]{1,0:T(8,128)(2,1)} %short_in.1) | copy-start | bytes 1572868
  1.4 14.1 %copy-start.8 = (bf16[1024,256]{1,0:T(8,128)(2,1)S(1)}, bf16[1024,256]{1,0:T(8,128)(2,1)}, u32[]{:S(2)}) copy-start(bf16[1024,256]{1,0:T(8,128)(2,1)} %short_out.1) | copy-start | bytes 1572868
  15.4 2.2 %copy-start.3 = (bf16[2,1024,1024]{2,1,0:T(8,128)(2,1)S(1)}, bf16[2,1024,1024]{2,1,0:T(8,128)(2,1)}, u32[]{:S(2)}) copy-start(bf16[2,1024,1024]{2,1,0:T(8,128)(2,1)} %short_mid.1) | copy-start | bytes 12582916
  17.6 17.8 %copy-start = (f32[96,48,128]{2,1,0:T(8,128)S(1)}, f32[96,48,128]{2,1,0:T(8,128)}, u32[]{:S(2)}) copy-start(f32[96,48,128]{2,1,0:T(8,128)} %courant_e.1) | copy-start | bytes 7077892
  17.6 17.8 %copy-start.4 = (bf16[2,1024,1024]{2,1,0:T(8,128)(2,1)S(1)}, bf16[2,1024,1024]{2,1,0:T(8,128)(2,1)}, u32[]{:S(2)}) copy-start(bf16[2,1024,1024]{2,1,0:T(8,128)(2,1)} %short_mid.1) | copy-start | bytes 12582916

commit v3 on v2

v3 whole, which is shorter than its diff:
```python
import functools

import jax
import jax.numpy as jnp
from jax import lax
from jax.experimental import pallas as pl
from jax.experimental.pallas import tpu as pltpu
from jax.sharding import PartitionSpec as P

BF16 = jnp.bfloat16
F32 = jnp.float32


def dot(a, b):
    return jnp.dot(a, b, preferred_element_type=F32)


def silu_of_twice(h):
    return (h + h * jnp.tanh(h)).astype(BF16)


def nets(half_cols, sun_col, w):
    long_in, long_out, short_in, short_sun, short_mid, short_out = w
    half_sun = sun_col * 0.5
    sun_row = short_sun[...]
    first = silu_of_twice(dot(half_cols, short_in[...]) + half_sun * sun_row)
    hidden = silu_of_twice(dot(half_cols, long_in[...]))
    second = silu_of_twice(dot(first, short_mid[0]) * 0.5)
    long_tend = dot(hidden, long_out[...])
    third = silu_of_twice(dot(second, short_mid[1]) * 0.5)
    short_tend = dot(third, short_out[...])
    return long_tend + jnp.where(sun_col > 0.0, short_tend, 0.0)


def lit_sun_column(day_ref, sun_ref, row0, rows):
    lit = jnp.where(day_ref[...] > 0, sun_ref[...], 0.0)
    lane = lax.broadcasted_iota(jnp.int32, lit.shape, 1)
    return jnp.concatenate(
        [
            jnp.sum(jnp.where(lane == row0 + r, lit, 0.0), axis=1, keepdims=True)
            for r in range(rows)
        ],
        axis=0,
    )


def pack_kernel(
    day_hbm, sun_hbm, short_sun_hbm, state, courant, out_a, out_b, sun_row,
    day, sun, short_sun, west, east, wind, sems,
):
    feats, levels = state.shape[-1], courant.shape[-1]
    end = feats + levels
    cells, lat_rows = day.shape
    copies = [
        pltpu.make_async_copy(src, dst, sems.at[k])
        for k, (src, dst) in enumerate((
            (state.at[:, pl.ds(0, 8), :], west),
            (state.at[:, pl.ds(cells - 8, 8), :], east),
            (courant.at[:, pl.ds(cells - 8, 8), :], wind),
            (day_hbm, day),
            (sun_hbm, sun),
            (short_sun_hbm, short_sun),
        ))
    ]
    for copy in copies:
        copy.start()
    for copy in copies[3:]:
        copy.wait()
    odd = lax.rem(lax.axis_index("lon"), 2) == 1
    lit = jnp.where(day[...] > 0, sun[...], 0.0)

    def choose(to_east, to_west):
        a, b = jnp.where(odd, to_west, to_east), jnp.where(odd, to_east, to_west)
        return a.astype(BF16), b.astype(BF16)

    sun_row[...] = short_sun[...].astype(F32).reshape(sun_row.shape)
    for out, row in zip((out_a, out_b), choose(lit[cells - 1 :], lit[:1])):
        out[:, end:] = jnp.zeros((lat_rows, out.shape[1] - end), BF16)
        out[:16, end : end + lat_rows] = jnp.broadcast_to(row, (16, lat_rows))
    for copy in copies[:3]:
        copy.wait()
    out_a[:, :feats], out_b[:, :feats] = choose(east[:, 7, :], west[:, 0, :])
    out_a[:, feats:end] = wind[:, 7, :].astype(BF16)
    out_b[:, feats:end] = wind[:, 7, :].astype(BF16)


def first_kernel(rows, day, sun, state, *rest):
    *w, tend, prov = rest
    row0 = pl.multiple_of(pl.program_id(0) * rows, rows)
    _, cells, feats = state.shape
    cols = rows * cells
    sun_col = lit_sun_column(day, sun, row0, rows)
    own = state[pl.ds(row0, rows)].reshape(cols, feats)
    phys = nets((own * 0.5).astype(BF16), sun_col, w)
    tend[0] = phys.astype(BF16).reshape(rows, cells, feats)
    prov[pl.ds(row0, rows)] = (own + phys).reshape(rows, cells, feats)


def transport(prov, courant, west_prov, west_cour, east_prov):
    rows, cells, feats = prov.shape
    cols = rows * cells
    pair = jnp.concatenate([courant, courant], axis=-1)
    east_wind, west_wind = jnp.maximum(pair, 0.0), jnp.minimum(pair, 0.0)
    sub = lax.broadcasted_iota(jnp.int32, (rows, 8, feats), 1)
    nxt = pltpu.roll(prov.reshape(cols, feats), cols - 1, 0).reshape(rows, cells, feats)
    tail = jnp.where(sub == 7, east_prov[:, None, :], nxt[:, cells - 8 :])
    nxt = jnp.concatenate([nxt[:, : cells - 8], tail], axis=1)
    flux = east_wind * prov + west_wind * nxt
    prev = pltpu.roll(flux.reshape(cols, feats), 1, 0).reshape(rows, cells, feats)
    wc = jnp.concatenate([west_cour, west_cour], axis=-1)
    face = (jnp.maximum(wc, 0.0) * west_prov)[:, None, :] + jnp.minimum(wc, 0.0)[:, None, :] * prov[:, :8]
    head = jnp.where(sub == 0, face, prev[:, :8])
    prev = jnp.concatenate([head, prev[:, 8:]], axis=1)
    return prov - (flux - prev)


def second_kernel(
    rows, day, sun, state, courant, halo_a, halo_b, prov_lo, tend_in,
    long_in, long_out, short_in, short_sun, short_mid, short_out,
    new_state, tend, prov, edges, west_wind,
):
    i = pl.program_id(0)
    tiles = pl.num_programs(0) - 1
    half = tiles * rows
    _, cells, feats = state.shape
    cols = rows * cells
    levels = courant.shape[-1]
    end = feats + levels
    lat_rows = day.shape[1]
    odd = lax.rem(lax.axis_index("lon"), 2) == 1

    def column_nets():
        lo = pl.multiple_of(i * rows, rows)
        hi = pl.multiple_of(half + i * rows, rows)

        def sides(at, n, lanes):
            a, b = halo_a[pl.ds(at, n), lanes].astype(F32), halo_b[pl.ds(at, n), lanes].astype(F32)
            return jnp.where(odd, a, b), jnp.where(odd, b, a)

        west_lo, east_lo = sides(lo, rows, slice(0, feats))
        west_hi, east_hi = sides(hi, rows, slice(0, feats))
        halos = [west_lo, west_hi, east_lo, east_hi]
        west_sun, east_sun = sides(0, 16, slice(end, end + 128))
        lane = lax.broadcasted_iota(jnp.int32, (rows, 128), 1)
        sub = lax.broadcasted_iota(jnp.int32, (rows, 128), 0)
        suns = [
            jnp.sum(jnp.where(lane == sub + at, lit, 0.0), axis=1, keepdims=True)
            for lit, at in ((west_sun, lo), (west_sun, hi), (east_sun, lo), (east_sun, hi))
        ]
        sun_all = jnp.concatenate([lit_sun_column(day, sun, hi, rows)] + suns, axis=0)
        own = state[pl.ds(hi, rows)].reshape(cols, feats)
        half_cols = (jnp.concatenate([own] + halos, axis=0) * 0.5).astype(BF16)
        phys = nets(half_cols, sun_all, (long_in, long_out, short_in, short_sun, short_mid, short_out))
        tend[0] = phys[:cols].astype(BF16).reshape(rows, cells, feats)
        prov[...] = (own + phys[:cols]).reshape(rows, cells, feats)
        edges[...] = jnp.concatenate(halos, axis=0) + phys[cols:]
        west_wind[:rows] = sides(lo, rows, slice(feats, end))[0]
        west_wind[rows:] = sides(hi, rows, slice(feats, end))[0]

    def move():
        lo = pl.multiple_of((i - 1) * rows, rows)
        new_state[0] = transport(
            prov_lo[pl.ds(lo, rows)], courant[pl.ds(lo, rows)],
            edges[:rows], west_wind[:rows], edges[2 * rows : 3 * rows],
        )
        new_state[1] = transport(
            prov[...], courant[pl.ds(half + lo, rows)],
            edges[rows : 2 * rows], west_wind[rows:], edges[3 * rows :],
        )

    @pl.when(i == 0)
    def _():
        column_nets()

    @pl.when(jnp.logical_and(i > 0, i < tiles))
    def _():
        move()
        column_nets()

    @pl.when(i == tiles)
    def _():
        move()


def shards(
    state, courant, daylit, insolation, long_in, long_out, short_in, short_sun, short_mid, short_out
):
    lat_rows, cells, feats = state.shape
    levels = courant.shape[-1]
    hid = long_in.shape[1]
    size = lax.axis_size("lon")
    rows = 16
    half = lat_rows // 2
    steps = half // rows
    width = feats + levels + 128
    day_t, sun_t = daylit.T, insolation.T
    in_vmem = pl.BlockSpec(memory_space=pltpu.VMEM)
    in_hbm = pl.BlockSpec(memory_space=pltpu.HBM)
    edge = pltpu.VMEM((lat_rows, width), BF16)
    edge_a, edge_b, sun_row = pl.pallas_call(
        pack_kernel,
        in_specs=[in_hbm] * 5,
        out_specs=(in_vmem,) * 3,
        out_shape=(edge, edge, pltpu.VMEM((1, hid), F32)),
        scratch_shapes=[
            pltpu.VMEM((cells, lat_rows), jnp.int32),
            pltpu.VMEM((cells, lat_rows), F32),
            pltpu.VMEM((hid,), BF16),
            pltpu.VMEM((lat_rows, 8, feats), F32),
            pltpu.VMEM((lat_rows, 8, feats), F32),
            pltpu.VMEM((lat_rows, 8, levels), F32),
            pltpu.SemaphoreType.DMA((6,)),
        ],
        compiler_params=pltpu.CompilerParams(vmem_limit_bytes=8 * 2**20),
        cost_estimate=pl.CostEstimate(flops=0, bytes_accessed=8 * 2**20, transcendentals=0),
        name="edges_packed",
    )(*(pltpu.with_memory_space_constraint(x, pltpu.HBM) for x in (day_t, sun_t, short_sun, state, courant)))
    flip = [(i, i ^ 1) for i in range(size)]
    seam = [(i, (i + 1 if i % 2 else i - 1) % size) for i in range(size)]
    halo_a = lax.ppermute(edge_a, "lon", flip)
    halo_b = lax.ppermute(edge_b, "lon", seam)

    def vmem(x):
        return pltpu.with_memory_space_constraint(x, pltpu.VMEM)

    weights = (vmem(long_in), vmem(long_out), vmem(short_in), sun_row, vmem(short_mid), vmem(short_out))
    macs = 4 * feats * hid + 2 * hid * hid
    params = pltpu.CompilerParams(vmem_limit_bytes=30 * 2**20)
    tend_shape = pltpu.HBM((2, half, cells, feats), BF16)
    v_state, v_day, v_sun = vmem(state), vmem(day_t), vmem(sun_t)
    tend, prov_lo = pl.pallas_call(
        functools.partial(first_kernel, rows),
        grid=(steps,),
        in_specs=[in_vmem] * 9,
        out_specs=(pl.BlockSpec((1, rows, cells, feats), lambda i: (0, i, 0, 0)), in_vmem),
        out_shape=(tend_shape, pltpu.VMEM((half, cells, feats), F32)),
        compiler_params=params,
        cost_estimate=pl.CostEstimate(
            flops=2 * half * cells * macs, bytes_accessed=2 * 2**20, transcendentals=0
        ),
        name="nets_first_half",
    )(v_day, v_sun, v_state, *weights)

    def here(i):
        return jnp.minimum(i, steps - 1)

    def before(i):
        return jnp.maximum(i - 1, 0)

    new_state, tend = pl.pallas_call(
        functools.partial(second_kernel, rows),
        grid=(steps + 1,),
        in_specs=[in_vmem] * 7 + [in_hbm] + [in_vmem] * 6,
        out_specs=(
            pl.BlockSpec((2, rows, cells, feats), lambda i: (0, before(i), 0, 0)),
            pl.BlockSpec((1, rows, cells, feats), lambda i: (1, here(i), 0, 0)),
        ),
        out_shape=(jax.ShapeDtypeStruct((2, half, cells, feats), F32), tend_shape),
        input_output_aliases={7: 1},
        scratch_shapes=[
            pltpu.VMEM((rows, cells, feats), F32),
            pltpu.VMEM((4 * rows, feats), F32),
            pltpu.VMEM((2 * rows, levels), F32),
        ],
        compiler_params=params,
        cost_estimate=pl.CostEstimate(
            flops=2 * half * (cells + 4) * macs, bytes_accessed=12 * 2**20, transcendentals=0
        ),
        name="nets_second_half_transport",
    )(v_day, v_sun, v_state, vmem(courant), vmem(halo_a), vmem(halo_b), vmem(prov_lo), tend, *weights)
    return new_state.reshape(state.shape), tend.reshape(state.shape)


def solution(mesh):
    in_specs = (
        P("ens", "lon", None),
        P("ens", "lon", None),
        P("ens", "lon"),
        P("ens", "lon"),
        P(),
        P(),
        P(),
        P(),
        P(),
        P(),
    )
    out_specs = (P("ens", "lon", None), P("ens", "lon", None))
    return jax.shard_map(shards, mesh=mesh, in_specs=in_specs, out_specs=out_specs, check_vma=False)
```

time: 58.5 us -> 48.9 us (0.84)
  blocking collectives: 11.1 us -> 0 us
  starting transfers between devices: 0 us -> 6.18 us
  Pallas kernels: 43.5 us -> 39.6 us
  local copies, waits for them, and re-layouts: 2.91 us -> 2.22 us
    all_gather x2 -> x0, blocking collectives: 11.1 us -> none  [the longest x1 8.89 us: exchange(): lax.all_gather(edge_b, 'lon', axis_index_groups=seams)]
    ppermute x0 -> x2, starting transfers between devices: none -> 6.18 us  [the longest x1 5.67 us: shards(): halo_b = lax.ppermute(edge_b, 'lon', seam)]
    pallas_call x1, Pallas kernels: 22.9 us -> 21 us  [shards(): pl.pallas_call(functools.partial(second_kernel, rows), grid=(steps + 1,),...]
    pallas_call x1, Pallas kernels: 17.8 us -> 16.6 us  [shards(): pl.pallas_call(functools.partial(first_kernel, rows), grid=(steps,), in_s...]
    pallas_call x1, Pallas kernels: 2.88 us -> 2.01 us  [shards(): pl.pallas_call(pack_kernel, in_specs=[in_hbm] * 5, out_specs=(in_vmem,) *...]
    reshape x1 -> x0, local copies, waits for them, and re-layouts: 0.69 us -> none  [shards(): short_sun.reshape(1, hid)]
    unnamed x18 -> x20, local copies, waits for them, and re-layouts: 2.22 us -> 2.22 us
  transfers between devices with their start and end apart: 0 -> 2, of which waited for: 0 -> 0; matrix products, arithmetic and copies ran while one was open for 0% -> 0% of each run, Pallas kernels for 0% -> 34%
where the time goes in v3:
time: 48.9 us; the launch traced here: 48.8 us
  Pallas kernels  39.6 us (81%)
  starting transfers between devices  6.18 us (13%)
  local copies, waits for them, and re-layouts  2.22 us (5%)
  between operations  0.75 us (2%)
    pallas_call x1, Pallas kernels, shards(): pl.pallas_call(functools.partial(second_kernel, rows), grid=(steps + 1,),...  21 us
    pallas_call x1, Pallas kernels, shards(): pl.pallas_call(functools.partial(first_kernel, rows), grid=(steps,), in_s...  16.6 us
    ppermute x1, starting transfers between devices, shards(): halo_b = lax.ppermute(edge_b, 'lon', seam)  5.67 us
    unnamed x20, local copies, waits for them, and re-layouts  2.22 us
    pallas_call x1, Pallas kernels, shards(): pl.pallas_call(pack_kernel, in_specs=[in_hbm] * 5, out_specs=(in_vmem,) *...  2.01 us
  transfers between devices with their start and end apart: 2, of which 0 were waited for; matrix products, arithmetic and copies ran while one was open for 0% of the time, Pallas kernels for 34%

profile of v3, /device:TPU:0, one launch (start us, length us, event | category | flops | bytes accessed | tf_op | source)
XLA Modules:
  0.0 48.8 jit_solution(10265716806338437575)
XLA Ops:
  0.6 0.0 copy-start
  0.6 0.0 copy-start.2
  0.7 0.0 copy-start.3
  0.7 0.0 copy-start.6
  0.7 0.0 copy-start.7
  0.7 0.0 copy-start.8
  0.7 0.0 copy-start.9
  0.7 2.0 %edges_packed.1 = (bf16[96,512]{1,0:T(8,128)(2,1)S(1)}, bf16[96,512]{1,0:T(8,128)(2,1)S(1)}, f32[1,1024]{1,0:T(1,128)S(1)}) custom-call(s32[48,96]{1,0:T(8,128)} %bitcast.4, f32[48,96]{1,0:T(8,128)} %bitcast.7, bf16[1024]{0:T(1024)(128)(2,1)} %short_sun_hbm.1, f32[96,48,256]{2,1,0:T(8,128)} %state.5, f32[96,48,128]{2,1,0:T(8,128)} %courant.3), custom_call_target="tpu_custom_call" | custom-call | bytes 8388608 | tf_op jit(solution)/shard_map/edges_packed/pallas_call | solution.py:200
  2.7 0.5 %collective-permute-start = (bf16[96,512]{1,0:T(8,128)(2,1)S(1)}, bf16[96,512]{1,0:T(8,128)(2,1)S(1)}, u32[]{:S(2)}, u32[]{:S(2)}) collective-permute-start(bf16[96,512]{1,0:T(8,128)(2,1)S(1)} %get-tuple-element.9), channel_id=1, source_target_pairs={{0,1},{1,0},{2,3},{3,2},{4,5},{5,4},{6,7},{7,6},{8,9},{9,8},{10,11... | collective-permute-start | bytes 294920 | tf_op jit(solution)/shard_map/ppermute | solution.py:220
  3.2 5.7 %collective-permute-start.1 = (bf16[96,512]{1,0:T(8,128)(2,1)S(1)}, bf16[96,512]{1,0:T(8,128)(2,1)S(1)}, u32[]{:S(2)}, u32[]{:S(2)}) collective-permute-start(bf16[96,512]{1,0:T(8,128)(2,1)S(1)} %get-tuple-element.10), channel_id=1, source_target_pairs={{0,15},{1,2},{2,1},{3,4},{4,3},{5,6},{6,5},{7,8},{8,7},{9,10},{10,... | collective-permute-start | bytes 294920 | tf_op jit(solution)/shard_map/ppermute | solution.py:221
  8.9 0.0 copy-done
  8.9 0.0 copy-done.2
  8.9 0.0 copy-done.3
  8.9 0.0 copy-done.6
  8.9 0.0 copy-done.7
  8.9 0.0 copy-done.8
  8.9 0.0 copy-done.9
  9.0 0.0 copy-start.4
  9.0 2.2 %copy-done.4 = bf16[2,1024,1024]{2,1,0:T(8,128)(2,1)S(1)} copy-done((bf16[2,1024,1024]{2,1,0:T(8,128)(2,1)S(1)}, bf16[2,1024,1024]{2,1,0:T(8,128)(2,1)}, u32[]{:S(2)}) %copy-start.4) | copy-done | bytes 4194328
  11.1 0.0 copy-start.1
  11.1 0.0 copy-start.5
  11.1 16.6 %nets_first_half.1 = (bf16[2,48,48,256]{3,2,1,0:T(8,128)(2,1)}, f32[48,48,256]{2,1,0:T(8,128)S(1)}) custom-call(s32[48,96]{1,0:T(8,128)S(1)} %bitcast.5, f32[48,96]{1,0:T(8,128)S(1)} %bitcast.8, f32[96,48,256]{2,1,0:T(8,128)S(1)} %copy-done, bf16[256,1024]{1,0:T(8,128)(2,1)S(1)} %copy-done.6, bf16[1024,256]{1,0:T(8,128)(2,1)S(1)} %copy-done.7, ...), custom_call_target="tpu_custom_call" | custom-call | flops 14495514624 | bytes 2097152 | tf_op jit(solution)/shard_map/nets_first_half/pallas_call | solution.py:231
  27.8 0.0 collective-permute-done.halo_a
  27.8 0.0 collective-permute-done.1.halo_b
  27.8 0.0 copy-done.1
  27.8 0.0 copy-done.5
  27.8 21.0 %nets_second_half_transport.1 = (f32[2,48,48,256]{3,2,1,0:T(8,128)}, bf16[2,48,48,256]{3,2,1,0:T(8,128)(2,1)}) custom-call(s32[48,96]{1,0:T(8,128)S(1)} %bitcast.6, f32[48,96]{1,0:T(8,128)S(1)} %bitcast.9, f32[96,48,256]{2,1,0:T(8,128)S(1)} %copy-done, f32[96,48,128]{2,1,0:T(8,128)S(1)} %copy-done.1, ...), custom_call_target="tpu_custom_call", output_to_operand_aliasing={{1}: (7, {})} | custom-call | flops 15703474176 | bytes 12582912 | tf_op jit(solution)/shard_map/nets_second_half_transport/pallas_call | solution.py:250
Async XLA Ops:
  0.6 8.3 %copy-start = (f32[96,48,256]{2,1,0:T(8,128)S(1)}, f32[96,48,256]{2,1,0:T(8,128)}, u32[]{:S(2)}) copy-start(f32[96,48,256]{2,1,0:T(8,128)} %state.5) | copy-start | bytes 14155780
  0.6 8.3 %copy-start.2 = (s32[96,48]{0,1:T(8,128)S(1)}, s32[96,48]{0,1:T(8,128)}, u32[]{:S(2)}) copy-start(s32[96,48]{0,1:T(8,128)} %param.12) | copy-start | bytes 55300
  0.7 8.3 %copy-start.3 = (f32[96,48]{0,1:T(8,128)S(1)}, f32[96,48]{0,1:T(8,128)}, u32[]{:S(2)}) copy-start(f32[96,48]{0,1:T(8,128)} %param.13) | copy-start | bytes 55300
  0.7 8.3 %copy-start.6 = (bf16[256,1024]{1,0:T(8,128)(2,1)S(1)}, bf16[256,1024]{1,0:T(8,128)(2,1)}, u32[]{:S(2)}) copy-start(bf16[256,1024]{1,0:T(8,128)(2,1)} %long_in.1) | copy-start | bytes 1572868
  0.7 8.3 %copy-start.7 = (bf16[1024,256]{1,0:T(8,128)(2,1)S(1)}, bf16[1024,256]{1,0:T(8,128)(2,1)}, u32[]{:S(2)}) copy-start(bf16[1024,256]{1,0:T(8,128)(2,1)} %long_out.1) | copy-start | bytes 1572868
  0.7 8.3 %copy-start.8 = (bf16[256,1024]{1,0:T(8,128)(2,1)S(1)}, bf16[256,1024]{1,0:T(8,128)(2,1)}, u32[]{:S(2)}) copy-start(bf16[256,1024]{1,0:T(8,128)(2,1)} %short_in.1) | copy-start | bytes 1572868
  0.7 8.3 %copy-start.9 = (bf16[1024,256]{1,0:T(8,128)(2,1)S(1)}, bf16[1024,256]{1,0:T(8,128)(2,1)}, u32[]{:S(2)}) copy-start(bf16[1024,256]{1,0:T(8,128)(2,1)} %short_out.1) | copy-start | bytes 1572868
  2.7 25.1 %collective-permute-start = (bf16[96,512]{1,0:T(8,128)(2,1)S(1)}, bf16[96,512]{1,0:T(8,128)(2,1)S(1)}, u32[]{:S(2)}, u32[]{:S(2)}) collective-permute-start(bf16[96,512]{1,0:T(8,128)(2,1)S(1)} %get-tuple-element.9), channel_id=1, source_target_pairs={{0,1},{1,0},{2,3},{3,2},{4,5},{5,4},{6,7},{7,6},{8,9},{9,8},{10,11... | collective-permute-start | bytes 294920 | tf_op jit(solution)/shard_map/ppermute | solution.py:220
  3.2 24.5 %collective-permute-start.1 = (bf16[96,512]{1,0:T(8,128)(2,1)S(1)}, bf16[96,512]{1,0:T(8,128)(2,1)S(1)}, u32[]{:S(2)}, u32[]{:S(2)}) collective-permute-start(bf16[96,512]{1,0:T(8,128)(2,1)S(1)} %get-tuple-element.10), channel_id=1, source_target_pairs={{0,15},{1,2},{2,1},{3,4},{4,3},{5,6},{6,5},{7,8},{8,7},{9,10},{10,... | collective-permute-start | bytes 294920 | tf_op jit(solution)/shard_map/ppermute | solution.py:221
  9.0 2.2 %copy-start.4 = (bf16[2,1024,1024]{2,1,0:T(8,128)(2,1)S(1)}, bf16[2,1024,1024]{2,1,0:T(8,128)(2,1)}, u32[]{:S(2)}) copy-start(bf16[2,1024,1024]{2,1,0:T(8,128)(2,1)} %short_mid.1) | copy-start | bytes 12582916
  11.1 16.6 %copy-start.1 = (f32[96,48,128]{2,1,0:T(8,128)S(1)}, f32[96,48,128]{2,1,0:T(8,128)}, u32[]{:S(2)}) copy-start(f32[96,48,128]{2,1,0:T(8,128)} %courant.3) | copy-start | bytes 7077892
  11.1 16.6 %copy-start.5 = (bf16[2,1024,1024]{2,1,0:T(8,128)(2,1)S(1)}, bf16[2,1024,1024]{2,1,0:T(8,128)(2,1)}, u32[]{:S(2)}) copy-start(bf16[2,1024,1024]{2,1,0:T(8,128)(2,1)} %short_mid.1) | copy-start | bytes 12582916

commit v4 on v3

--- a/solution.py
+++ b/solution.py
@@ -54,9 +54,9 @@
     copies = [
         pltpu.make_async_copy(src, dst, sems.at[k])
         for k, (src, dst) in enumerate((
-            (state.at[:, pl.ds(0, 8), :], west),
-            (state.at[:, pl.ds(cells - 8, 8), :], east),
-            (courant.at[:, pl.ds(cells - 8, 8), :], wind),
+            (state.at[:, pl.ds(0, 1), :], west),
+            (state.at[:, pl.ds(cells - 1, 1), :], east),
+            (courant.at[:, pl.ds(cells - 1, 1), :], wind),
             (day_hbm, day),
             (sun_hbm, sun),
             (short_sun_hbm, short_sun),
@@ -79,9 +79,9 @@
         out[:16, end : end + lat_rows] = jnp.broadcast_to(row, (16, lat_rows))
     for copy in copies[:3]:
         copy.wait()
-    out_a[:, :feats], out_b[:, :feats] = choose(east[:, 7, :], west[:, 0, :])
-    out_a[:, feats:end] = wind[:, 7, :].astype(BF16)
-    out_b[:, feats:end] = wind[:, 7, :].astype(BF16)
+    out_a[:, :feats], out_b[:, :feats] = choose(east[:, 0, :], west[:, 0, :])
+    out_a[:, feats:end] = wind[:, 0, :].astype(BF16)
+    out_b[:, feats:end] = wind[:, 0, :].astype(BF16)
 
 
 def first_kernel(rows, day, sun, state, *rest):
@@ -206,13 +206,13 @@
             pltpu.VMEM((cells, lat_rows), jnp.int32),
             pltpu.VMEM((cells, lat_rows), F32),
             pltpu.VMEM((hid,), BF16),
-            pltpu.VMEM((lat_rows, 8, feats), F32),
-            pltpu.VMEM((lat_rows, 8, feats), F32),
-            pltpu.VMEM((lat_rows, 8, levels), F32),
+            pltpu.VMEM((lat_rows, 1, feats), F32),
+            pltpu.VMEM((lat_rows, 1, feats), F32),
+            pltpu.VMEM((lat_rows, 1, levels), F32),
             pltpu.SemaphoreType.DMA((6,)),
         ],
         compiler_params=pltpu.CompilerParams(vmem_limit_bytes=8 * 2**20),
-        cost_estimate=pl.CostEstimate(flops=0, bytes_accessed=8 * 2**20, transcendentals=0),
+        cost_estimate=pl.CostEstimate(flops=8 * 10**9, bytes_accessed=8 * 2**20, transcendentals=0),
         name="edges_packed",
     )(*(pltpu.with_memory_space_constraint(x, pltpu.HBM) for x in (day_t, sun_t, short_sun, state, courant)))
     flip = [(i, i ^ 1) for i in range(size)]

time: 48.9 us -> 46 us (0.941)
  local copies, waits for them, and re-layouts: 2.22 us -> 0.04 us
  Pallas kernels: 39.6 us -> 38.8 us
    unnamed x20 -> x18, local copies, waits for them, and re-layouts: 2.22 us -> 0.04 us
    pallas_call x1, Pallas kernels: 2.01 us -> 1.49 us  [shards(): pl.pallas_call(pack_kernel, in_specs=[in_hbm] * 5, out_specs=(in_vmem,) *...]
  transfers between devices with their start and end apart: 2 -> 2, of which waited for: 0 -> 0; matrix products, arithmetic and copies ran while one was open for 0% -> 0% of each run, Pallas kernels for 34% -> 36%
where the time goes in v4:
time: 46 us; the launch traced here: 45.8 us
  Pallas kernels  38.8 us (84%)
  starting transfers between devices  6.18 us (13%)
  between operations  0.75 us (2%)
    pallas_call x1, Pallas kernels, shards(): pl.pallas_call(functools.partial(second_kernel, rows), grid=(steps + 1,),...  20.8 us
    pallas_call x1, Pallas kernels, shards(): pl.pallas_call(functools.partial(first_kernel, rows), grid=(steps,), in_s...  16.5 us
    ppermute x1, starting transfers between devices, shards(): halo_b = lax.ppermute(edge_b, 'lon', seam)  5.67 us
    pallas_call x1, Pallas kernels, shards(): pl.pallas_call(pack_kernel, in_specs=[in_hbm] * 5, out_specs=(in_vmem,) *...  1.49 us
  transfers between devices with their start and end apart: 2, of which 0 were waited for; matrix products, arithmetic and copies ran while one was open for 0% of the time, Pallas kernels for 36%

profile of v4, /device:TPU:0, one launch (start us, length us, event | category | flops | bytes accessed | tf_op | source)
XLA Modules:
  0.0 45.8 jit_solution(12063381882427841503)
XLA Ops:
  0.6 0.0 copy-start
  0.6 0.0 copy-start.1
  0.7 0.0 copy-start.3
  0.7 0.0 copy-start.4
  0.7 0.0 copy-start.5
  0.7 0.0 copy-start.6
  0.7 0.0 copy-start.7
  0.7 0.0 copy-start.8
  0.7 1.5 %edges_packed.1 = (bf16[96,512]{1,0:T(8,128)(2,1)S(1)}, bf16[96,512]{1,0:T(8,128)(2,1)S(1)}, f32[1,1024]{1,0:T(1,128)S(1)}) custom-call(s32[48,96]{1,0:T(8,128)} %bitcast.4, f32[48,96]{1,0:T(8,128)} %bitcast.7, bf16[1024]{0:T(1024)(128)(2,1)} %short_sun_hbm.1, f32[96,48,256]{2,1,0:T(8,128)} %state.5, f32[96,48,128]{2,1,0:T(8,128)} %courant.3), custom_call_target="tpu_custom_call" | custom-call | flops 8000000000 | bytes 8388608 | tf_op jit(solution)/shard_map/edges_packed/pallas_call | solution.py:200
  2.2 0.5 %collective-permute-start = (bf16[96,512]{1,0:T(8,128)(2,1)S(1)}, bf16[96,512]{1,0:T(8,128)(2,1)S(1)}, u32[]{:S(2)}, u32[]{:S(2)}) collective-permute-start(bf16[96,512]{1,0:T(8,128)(2,1)S(1)} %get-tuple-element.9), channel_id=1, source_target_pairs={{0,1},{1,0},{2,3},{3,2},{4,5},{5,4},{6,7},{7,6},{8,9},{9,8},{10,11... | collective-permute-start | bytes 294920 | tf_op jit(solution)/shard_map/ppermute | solution.py:220
  2.7 5.7 %collective-permute-start.1 = (bf16[96,512]{1,0:T(8,128)(2,1)S(1)}, bf16[96,512]{1,0:T(8,128)(2,1)S(1)}, u32[]{:S(2)}, u32[]{:S(2)}) collective-permute-start(bf16[96,512]{1,0:T(8,128)(2,1)S(1)} %get-tuple-element.10), channel_id=1, source_target_pairs={{0,15},{1,2},{2,1},{3,4},{4,3},{5,6},{6,5},{7,8},{8,7},{9,10},{10,... | collective-permute-start | bytes 294920 | tf_op jit(solution)/shard_map/ppermute | solution.py:221
  8.4 0.0 copy-done
  8.4 0.0 copy-done.1
  8.4 0.0 copy-done.3
  8.4 0.0 copy-done.4
  8.4 0.0 copy-done.5
  8.4 0.0 copy-done.6
  8.4 0.0 copy-done.7
  8.4 0.0 copy-done.8
  8.5 0.0 copy-start.2
  8.5 16.5 %nets_first_half.1 = (bf16[2,48,48,256]{3,2,1,0:T(8,128)(2,1)}, f32[48,48,256]{2,1,0:T(8,128)S(1)}) custom-call(s32[48,96]{1,0:T(8,128)S(1)} %bitcast.5, f32[48,96]{1,0:T(8,128)S(1)} %bitcast.8, f32[96,48,256]{2,1,0:T(8,128)S(1)} %copy-done, bf16[256,1024]{1,0:T(8,128)(2,1)S(1)} %copy-done.3, bf16[1024,256]{1,0:T(8,128)(2,1)S(1)} %copy-done.4, ...), custom_call_target="tpu_custom_call" | custom-call | flops 14495514624 | bytes 2097152 | tf_op jit(solution)/shard_map/nets_first_half/pallas_call | solution.py:231
  24.9 0.0 collective-permute-done.halo_a
  24.9 0.0 collective-permute-done.1.halo_b
  24.9 0.0 copy-done.2
  24.9 20.8 %nets_second_half_transport.1 = (f32[2,48,48,256]{3,2,1,0:T(8,128)}, bf16[2,48,48,256]{3,2,1,0:T(8,128)(2,1)}) custom-call(s32[48,96]{1,0:T(8,128)S(1)} %bitcast.6, f32[48,96]{1,0:T(8,128)S(1)} %bitcast.9, f32[96,48,256]{2,1,0:T(8,128)S(1)} %copy-done, f32[96,48,128]{2,1,0:T(8,128)S(1)} %copy-done.2, ...), custom_call_target="tpu_custom_call", output_to_operand_aliasing={{1}: (7, {})} | custom-call | flops 15703474176 | bytes 12582912 | tf_op jit(solution)/shard_map/nets_second_half_transport/pallas_call | solution.py:250
Async XLA Ops:
  0.6 7.8 %copy-start = (f32[96,48,256]{2,1,0:T(8,128)S(1)}, f32[96,48,256]{2,1,0:T(8,128)}, u32[]{:S(2)}) copy-start(f32[96,48,256]{2,1,0:T(8,128)} %state.5) | copy-start | bytes 14155780
  0.6 7.8 %copy-start.1 = (bf16[2,1024,1024]{2,1,0:T(8,128)(2,1)S(1)}, bf16[2,1024,1024]{2,1,0:T(8,128)(2,1)}, u32[]{:S(2)}) copy-start(bf16[2,1024,1024]{2,1,0:T(8,128)(2,1)} %short_mid.1) | copy-start | bytes 12582916
  0.7 7.8 %copy-start.3 = (bf16[256,1024]{1,0:T(8,128)(2,1)S(1)}, bf16[256,1024]{1,0:T(8,128)(2,1)}, u32[]{:S(2)}) copy-start(bf16[256,1024]{1,0:T(8,128)(2,1)} %long_in.1) | copy-start | bytes 1572868
  0.7 7.7 %copy-start.4 = (bf16[1024,256]{1,0:T(8,128)(2,1)S(1)}, bf16[1024,256]{1,0:T(8,128)(2,1)}, u32[]{:S(2)}) copy-start(bf16[1024,256]{1,0:T(8,128)(2,1)} %long_out.1) | copy-start | bytes 1572868
  0.7 7.7 %copy-start.5 = (bf16[256,1024]{1,0:T(8,128)(2,1)S(1)}, bf16[256,1024]{1,0:T(8,128)(2,1)}, u32[]{:S(2)}) copy-start(bf16[256,1024]{1,0:T(8,128)(2,1)} %short_in.1) | copy-start | bytes 1572868
  0.7 7.7 %copy-start.6 = (bf16[1024,256]{1,0:T(8,128)(2,1)S(1)}, bf16[1024,256]{1,0:T(8,128)(2,1)}, u32[]{:S(2)}) copy-start(bf16[1024,256]{1,0:T(8,128)(2,1)} %short_out.1) | copy-start | bytes 1572868
  0.7 7.7 %copy-start.7 = (s32[96,48]{0,1:T(8,128)S(1)}, s32[96,48]{0,1:T(8,128)}, u32[]{:S(2)}) copy-start(s32[96,48]{0,1:T(8,128)} %param.12) | copy-start | bytes 55300
  0.7 7.7 %copy-start.8 = (f32[96,48]{0,1:T(8,128)S(1)}, f32[96,48]{0,1:T(8,128)}, u32[]{:S(2)}) copy-start(f32[96,48]{0,1:T(8,128)} %param.13) | copy-start | bytes 55300
  2.2 22.7 %collective-permute-start = (bf16[96,512]{1,0:T(8,128)(2,1)S(1)}, bf16[96,512]{1,0:T(8,128)(2,1)S(1)}, u32[]{:S(2)}, u32[]{:S(2)}) collective-permute-start(bf16[96,512]{1,0:T(8,128)(2,1)S(1)} %get-tuple-element.9), channel_id=1, source_target_pairs={{0,1},{1,0},{2,3},{3,2},{4,5},{5,4},{6,7},{7,6},{8,9},{9,8},{10,11... | collective-permute-start | bytes 294920 | tf_op jit(solution)/shard_map/ppermute | solution.py:220
  2.7 22.2 %collective-permute-start.1 = (bf16[96,512]{1,0:T(8,128)(2,1)S(1)}, bf16[96,512]{1,0:T(8,128)(2,1)S(1)}, u32[]{:S(2)}, u32[]{:S(2)}) collective-permute-start(bf16[96,512]{1,0:T(8,128)(2,1)S(1)} %get-tuple-element.10), channel_id=1, source_target_pairs={{0,15},{1,2},{2,1},{3,4},{4,3},{5,6},{6,5},{7,8},{8,7},{9,10},{10,... | collective-permute-start | bytes 294920 | tf_op jit(solution)/shard_map/ppermute | solution.py:221
  8.5 16.5 %copy-start.2 = (f32[96,48,128]{2,1,0:T(8,128)S(1)}, f32[96,48,128]{2,1,0:T(8,128)}, u32[]{:S(2)}) copy-start(f32[96,48,128]{2,1,0:T(8,128)} %courant.3) | copy-start | bytes 7077892

commit v5 on v4

--- a/solution.py
+++ b/solution.py
@@ -45,7 +45,7 @@
 
 
 def pack_kernel(
-    day_hbm, sun_hbm, short_sun_hbm, state, courant, out_a, out_b, sun_row,
+    day_hbm, sun_hbm, short_sun_hbm, state, courant, out_b, out_a, sun_row,
     day, sun, short_sun, west, east, wind, sems,
 ):
     feats, levels = state.shape[-1], courant.shape[-1]
@@ -115,7 +115,7 @@
 
 
 def second_kernel(
-    rows, day, sun, state, courant, halo_a, halo_b, prov_lo, tend_in,
+    rows, day, sun, state, courant, halo_b, halo_a, prov_lo, tend_in,
     long_in, long_out, short_in, short_sun, short_mid, short_out,
     new_state, tend, prov, edges, west_wind,
 ):
@@ -197,7 +197,7 @@
     in_vmem = pl.BlockSpec(memory_space=pltpu.VMEM)
     in_hbm = pl.BlockSpec(memory_space=pltpu.HBM)
     edge = pltpu.VMEM((lat_rows, width), BF16)
-    edge_a, edge_b, sun_row = pl.pallas_call(
+    edge_b, edge_a, sun_row = pl.pallas_call(
         pack_kernel,
         in_specs=[in_hbm] * 5,
         out_specs=(in_vmem,) * 3,
@@ -217,8 +217,8 @@
     )(*(pltpu.with_memory_space_constraint(x, pltpu.HBM) for x in (day_t, sun_t, short_sun, state, courant)))
     flip = [(i, i ^ 1) for i in range(size)]
     seam = [(i, (i + 1 if i % 2 else i - 1) % size) for i in range(size)]
+    halo_b = lax.ppermute(edge_b, "lon", seam)
     halo_a = lax.ppermute(edge_a, "lon", flip)
-    halo_b = lax.ppermute(edge_b, "lon", seam)
 
     def vmem(x):
         return pltpu.with_memory_space_constraint(x, pltpu.VMEM)
@@ -267,7 +267,7 @@
             flops=2 * half * (cells + 4) * macs, bytes_accessed=12 * 2**20, transcendentals=0
         ),
         name="nets_second_half_transport",
-    )(v_day, v_sun, v_state, vmem(courant), vmem(halo_a), vmem(halo_b), vmem(prov_lo), tend, *weights)
+    )(v_day, v_sun, v_state, vmem(courant), vmem(halo_b), vmem(halo_a), vmem(prov_lo), tend, *weights)
     return new_state.reshape(state.shape), tend.reshape(state.shape)
 
 

time: 46 us -> 45.3 us (0.985)
  starting transfers between devices: 6.18 us -> 5.51 us
    ppermute x1, starting transfers between devices: 0.52 us -> 0.01 us  [shards(): halo_a = lax.ppermute(edge_a, 'lon', flip)]
  transfers between devices with their start and end apart: 2 -> 2, of which waited for: 0 -> 0; matrix products, arithmetic and copies ran while one was open for 0% -> 0% of each run, Pallas kernels for 36% -> 37%
where the time goes in v5:
time: 45.3 us; the launch traced here: 45.1 us
  Pallas kernels  38.8 us (86%)
  starting transfers between devices  5.51 us (12%)
  between operations  0.77 us (2%)
    pallas_call x1, Pallas kernels, shards(): pl.pallas_call(functools.partial(second_kernel, rows), grid=(steps + 1,),...  20.8 us
    pallas_call x1, Pallas kernels, shards(): pl.pallas_call(functools.partial(first_kernel, rows), grid=(steps,), in_s...  16.5 us
    ppermute x1, starting transfers between devices, shards(): halo_b = lax.ppermute(edge_b, 'lon', seam)  5.51 us
    pallas_call x1, Pallas kernels, shards(): pl.pallas_call(pack_kernel, in_specs=[in_hbm] * 5, out_specs=(in_vmem,) *...  1.49 us
  transfers between devices with their start and end apart: 2, of which 0 were waited for; matrix products, arithmetic and copies ran while one was open for 0% of the time, Pallas kernels for 37%

profile of v5, /device:TPU:0, one launch (start us, length us, event | category | flops | bytes accessed | tf_op | source)
XLA Modules:
  0.0 45.1 jit_solution(9059369916685257194)
XLA Ops:
  0.6 0.0 copy-start
  0.6 0.0 copy-start.1
  0.7 0.0 copy-start.3
  0.7 0.0 copy-start.4
  0.7 0.0 copy-start.5
  0.7 0.0 copy-start.6
  0.7 0.0 copy-start.7
  0.7 0.0 copy-start.8
  0.7 1.5 %edges_packed.1 = (bf16[96,512]{1,0:T(8,128)(2,1)S(1)}, bf16[96,512]{1,0:T(8,128)(2,1)S(1)}, f32[1,1024]{1,0:T(1,128)S(1)}) custom-call(s32[48,96]{1,0:T(8,128)} %bitcast.4, f32[48,96]{1,0:T(8,128)} %bitcast.7, bf16[1024]{0:T(1024)(128)(2,1)} %short_sun_hbm.1, f32[96,48,256]{2,1,0:T(8,128)} %state.5, f32[96,48,128]{2,1,0:T(8,128)} %courant.3), custom_call_target="tpu_custom_call" | custom-call | flops 8000000000 | bytes 8388608 | tf_op jit(solution)/shard_map/edges_packed/pallas_call | solution.py:200
  2.2 5.5 %collective-permute-start = (bf16[96,512]{1,0:T(8,128)(2,1)S(1)}, bf16[96,512]{1,0:T(8,128)(2,1)S(1)}, u32[]{:S(2)}, u32[]{:S(2)}) collective-permute-start(bf16[96,512]{1,0:T(8,128)(2,1)S(1)} %get-tuple-element.9), channel_id=1, source_target_pairs={{0,15},{1,2},{2,1},{3,4},{4,3},{5,6},{6,5},{7,8},{8,7},{9,10},{10,... | collective-permute-start | bytes 294920 | tf_op jit(solution)/shard_map/ppermute | solution.py:220
  7.7 0.0 collective-permute-start.1
  7.7 0.0 copy-done
  7.7 0.0 copy-done.1
  7.7 0.0 copy-done.3
  7.7 0.0 copy-done.4
  7.8 0.0 copy-done.5
  7.8 0.0 copy-done.6
  7.8 0.0 copy-done.7
  7.8 0.0 copy-done.8
  7.8 0.0 copy-start.2
  7.8 16.5 %nets_first_half.1 = (bf16[2,48,48,256]{3,2,1,0:T(8,128)(2,1)}, f32[48,48,256]{2,1,0:T(8,128)S(1)}) custom-call(s32[48,96]{1,0:T(8,128)S(1)} %bitcast.5, f32[48,96]{1,0:T(8,128)S(1)} %bitcast.8, f32[96,48,256]{2,1,0:T(8,128)S(1)} %copy-done, bf16[256,1024]{1,0:T(8,128)(2,1)S(1)} %copy-done.3, bf16[1024,256]{1,0:T(8,128)(2,1)S(1)} %copy-done.4, ...), custom_call_target="tpu_custom_call" | custom-call | flops 14495514624 | bytes 2097152 | tf_op jit(solution)/shard_map/nets_first_half/pallas_call | solution.py:231
  24.3 0.0 collective-permute-done.halo_b
  24.3 0.0 collective-permute-done.1.halo_a
  24.3 0.0 copy-done.2
  24.3 20.8 %nets_second_half_transport.1 = (f32[2,48,48,256]{3,2,1,0:T(8,128)}, bf16[2,48,48,256]{3,2,1,0:T(8,128)(2,1)}) custom-call(s32[48,96]{1,0:T(8,128)S(1)} %bitcast.6, f32[48,96]{1,0:T(8,128)S(1)} %bitcast.9, f32[96,48,256]{2,1,0:T(8,128)S(1)} %copy-done, f32[96,48,128]{2,1,0:T(8,128)S(1)} %copy-done.2, ...), custom_call_target="tpu_custom_call", output_to_operand_aliasing={{1}: (7, {})} | custom-call | flops 15703474176 | bytes 12582912 | tf_op jit(solution)/shard_map/nets_second_half_transport/pallas_call | solution.py:250
Async XLA Ops:
  0.6 7.1 %copy-start = (f32[96,48,256]{2,1,0:T(8,128)S(1)}, f32[96,48,256]{2,1,0:T(8,128)}, u32[]{:S(2)}) copy-start(f32[96,48,256]{2,1,0:T(8,128)} %state.5) | copy-start | bytes 14155780
  0.6 7.1 %copy-start.1 = (bf16[2,1024,1024]{2,1,0:T(8,128)(2,1)S(1)}, bf16[2,1024,1024]{2,1,0:T(8,128)(2,1)}, u32[]{:S(2)}) copy-start(bf16[2,1024,1024]{2,1,0:T(8,128)(2,1)} %short_mid.1) | copy-start | bytes 12582916
  0.7 7.1 %copy-start.3 = (bf16[256,1024]{1,0:T(8,128)(2,1)S(1)}, bf16[256,1024]{1,0:T(8,128)(2,1)}, u32[]{:S(2)}) copy-start(bf16[256,1024]{1,0:T(8,128)(2,1)} %long_in.1) | copy-start | bytes 1572868
  0.7 7.1 %copy-start.4 = (bf16[1024,256]{1,0:T(8,128)(2,1)S(1)}, bf16[1024,256]{1,0:T(8,128)(2,1)}, u32[]{:S(2)}) copy-start(bf16[1024,256]{1,0:T(8,128)(2,1)} %long_out.1) | copy-start | bytes 1572868
  0.7 7.1 %copy-start.5 = (bf16[256,1024]{1,0:T(8,128)(2,1)S(1)}, bf16[256,1024]{1,0:T(8,128)(2,1)}, u32[]{:S(2)}) copy-start(bf16[256,1024]{1,0:T(8,128)(2,1)} %short_in.1) | copy-start | bytes 1572868
  0.7 7.1 %copy-start.6 = (bf16[1024,256]{1,0:T(8,128)(2,1)S(1)}, bf16[1024,256]{1,0:T(8,128)(2,1)}, u32[]{:S(2)}) copy-start(bf16[1024,256]{1,0:T(8,128)(2,1)} %short_out.1) | copy-start | bytes 1572868
  0.7 7.1 %copy-start.7 = (s32[96,48]{0,1:T(8,128)S(1)}, s32[96,48]{0,1:T(8,128)}, u32[]{:S(2)}) copy-start(s32[96,48]{0,1:T(8,128)} %param.12) | copy-start | bytes 55300
  0.7 7.1 %copy-start.8 = (f32[96,48]{0,1:T(8,128)S(1)}, f32[96,48]{0,1:T(8,128)}, u32[]{:S(2)}) copy-start(f32[96,48]{0,1:T(8,128)} %param.13) | copy-start | bytes 55300
  2.2 22.1 %collective-permute-start = (bf16[96,512]{1,0:T(8,128)(2,1)S(1)}, bf16[96,512]{1,0:T(8,128)(2,1)S(1)}, u32[]{:S(2)}, u32[]{:S(2)}) collective-permute-start(bf16[96,512]{1,0:T(8,128)(2,1)S(1)} %get-tuple-element.9), channel_id=1, source_target_pairs={{0,15},{1,2},{2,1},{3,4},{4,3},{5,6},{6,5},{7,8},{8,7},{9,10},{10,... | collective-permute-start | bytes 294920 | tf_op jit(solution)/shard_map/ppermute | solution.py:220
  7.7 16.6 %collective-permute-start.1 = (bf16[96,512]{1,0:T(8,128)(2,1)S(1)}, bf16[96,512]{1,0:T(8,128)(2,1)S(1)}, u32[]{:S(2)}, u32[]{:S(2)}) collective-permute-start(bf16[96,512]{1,0:T(8,128)(2,1)S(1)} %get-tuple-element.10), channel_id=1, source_target_pairs={{0,1},{1,0},{2,3},{3,2},{4,5},{5,4},{6,7},{7,6},{8,9},{9,8},{10,11... | collective-permute-start | bytes 294920 | tf_op jit(solution)/shard_map/ppermute | solution.py:221
  7.8 16.5 %copy-start.2 = (f32[96,48,128]{2,1,0:T(8,128)S(1)}, f32[96,48,128]{2,1,0:T(8,128)}, u32[]{:S(2)}) copy-start(f32[96,48,128]{2,1,0:T(8,128)} %courant.3) | copy-start | bytes 7077892

commit v6 on v5

--- a/solution.py
+++ b/solution.py
@@ -99,16 +99,23 @@
 def transport(prov, courant, west_prov, west_cour, east_prov):
     rows, cells, feats = prov.shape
     cols = rows * cells
-    pair = jnp.concatenate([courant, courant], axis=-1)
-    east_wind, west_wind = jnp.maximum(pair, 0.0), jnp.minimum(pair, 0.0)
+    levels = courant.shape[-1]
+    eastward = courant > 0.0
+
+    def upwind(wind, mask, here, there):
+        return jnp.concatenate(
+            [wind * jnp.where(mask, here[..., k : k + levels], there[..., k : k + levels]) for k in (0, levels)], axis=-1
+        )
+
     sub = lax.broadcasted_iota(jnp.int32, (rows, 8, feats), 1)
     nxt = pltpu.roll(prov.reshape(cols, feats), cols - 1, 0).reshape(rows, cells, feats)
     tail = jnp.where(sub == 7, east_prov[:, None, :], nxt[:, cells - 8 :])
     nxt = jnp.concatenate([nxt[:, : cells - 8], tail], axis=1)
-    flux = east_wind * prov + west_wind * nxt
+    flux = upwind(courant, eastward, prov, nxt)
     prev = pltpu.roll(flux.reshape(cols, feats), 1, 0).reshape(rows, cells, feats)
-    wc = jnp.concatenate([west_cour, west_cour], axis=-1)
-    face = (jnp.maximum(wc, 0.0) * west_prov)[:, None, :] + jnp.minimum(wc, 0.0)[:, None, :] * prov[:, :8]
+    west_wind = jnp.broadcast_to(west_cour[:, None, :], (rows, 8, levels))
+    west_here = jnp.broadcast_to(west_prov[:, None, :], (rows, 8, feats))
+    face = upwind(west_wind, west_wind > 0.0, west_here, prov[:, :8])
     head = jnp.where(sub == 0, face, prev[:, :8])
     prev = jnp.concatenate([head, prev[:, 8:]], axis=1)
     return prov - (flux - prev)

time: 45.3 us -> 45.1 us (level)
  no operation moved by 1% of the time
where the time goes in v6:
time: 45.1 us; the launch traced here: 44.9 us
  Pallas kernels  38.6 us (86%)
  starting transfers between devices  5.51 us (12%)
  between operations  0.77 us (2%)
    pallas_call x1, Pallas kernels, shards(): pl.pallas_call(functools.partial(second_kernel, rows), grid=(steps + 1,),...  20.6 us
    pallas_call x1, Pallas kernels, shards(): pl.pallas_call(functools.partial(first_kernel, rows), grid=(steps,), in_s...  16.5 us
    ppermute x1, starting transfers between devices, shards(): halo_b = lax.ppermute(edge_b, 'lon', seam)  5.51 us
    pallas_call x1, Pallas kernels, shards(): pl.pallas_call(pack_kernel, in_specs=[in_hbm] * 5, out_specs=(in_vmem,) *...  1.49 us
  transfers between devices with their start and end apart: 2, of which 0 were waited for; matrix products, arithmetic and copies ran while one was open for 0% of the time, Pallas kernels for 37%

profile of v6, /device:TPU:0, one launch (start us, length us, event | category | flops | bytes accessed | tf_op | source)
XLA Modules:
  0.0 44.9 jit_solution(4875690706509162738)
XLA Ops:
  0.6 0.0 copy-start
  0.6 0.0 copy-start.1
  0.7 0.0 copy-start.3
  0.7 0.0 copy-start.4
  0.7 0.0 copy-start.5
  0.7 0.0 copy-start.6
  0.7 0.0 copy-start.7
  0.7 0.0 copy-start.8
  0.7 1.5 %edges_packed.1 = (bf16[96,512]{1,0:T(8,128)(2,1)S(1)}, bf16[96,512]{1,0:T(8,128)(2,1)S(1)}, f32[1,1024]{1,0:T(1,128)S(1)}) custom-call(s32[48,96]{1,0:T(8,128)} %bitcast.4, f32[48,96]{1,0:T(8,128)} %bitcast.7, bf16[1024]{0:T(1024)(128)(2,1)} %short_sun_hbm.1, f32[96,48,256]{2,1,0:T(8,128)} %state.5, f32[96,48,128]{2,1,0:T(8,128)} %courant.3), custom_call_target="tpu_custom_call" | custom-call | flops 8000000000 | bytes 8388608 | tf_op jit(solution)/shard_map/edges_packed/pallas_call | solution.py:207
  2.2 5.5 %collective-permute-start = (bf16[96,512]{1,0:T(8,128)(2,1)S(1)}, bf16[96,512]{1,0:T(8,128)(2,1)S(1)}, u32[]{:S(2)}, u32[]{:S(2)}) collective-permute-start(bf16[96,512]{1,0:T(8,128)(2,1)S(1)} %get-tuple-element.9), channel_id=1, source_target_pairs={{0,15},{1,2},{2,1},{3,4},{4,3},{5,6},{6,5},{7,8},{8,7},{9,10},{10,... | collective-permute-start | bytes 294920 | tf_op jit(solution)/shard_map/ppermute | solution.py:227
  7.7 0.0 collective-permute-start.1
  7.7 0.0 copy-done
  7.7 0.0 copy-done.1
  7.7 0.0 copy-done.3
  7.7 0.0 copy-done.4
  7.8 0.0 copy-done.5
  7.8 0.0 copy-done.6
  7.8 0.0 copy-done.7
  7.8 0.0 copy-done.8
  7.8 0.0 copy-start.2
  7.8 16.5 %nets_first_half.1 = (bf16[2,48,48,256]{3,2,1,0:T(8,128)(2,1)}, f32[48,48,256]{2,1,0:T(8,128)S(1)}) custom-call(s32[48,96]{1,0:T(8,128)S(1)} %bitcast.5, f32[48,96]{1,0:T(8,128)S(1)} %bitcast.8, f32[96,48,256]{2,1,0:T(8,128)S(1)} %copy-done, bf16[256,1024]{1,0:T(8,128)(2,1)S(1)} %copy-done.3, bf16[1024,256]{1,0:T(8,128)(2,1)S(1)} %copy-done.4, ...), custom_call_target="tpu_custom_call" | custom-call | flops 14495514624 | bytes 2097152 | tf_op jit(solution)/shard_map/nets_first_half/pallas_call | solution.py:238
  24.3 0.0 collective-permute-done.halo_b
  24.3 0.0 collective-permute-done.1.halo_a
  24.3 0.0 copy-done.2
  24.3 20.6 %nets_second_half_transport.1 = (f32[2,48,48,256]{3,2,1,0:T(8,128)}, bf16[2,48,48,256]{3,2,1,0:T(8,128)(2,1)}) custom-call(s32[48,96]{1,0:T(8,128)S(1)} %bitcast.6, f32[48,96]{1,0:T(8,128)S(1)} %bitcast.9, f32[96,48,256]{2,1,0:T(8,128)S(1)} %copy-done, f32[96,48,128]{2,1,0:T(8,128)S(1)} %copy-done.2, ...), custom_call_target="tpu_custom_call", output_to_operand_aliasing={{1}: (7, {})} | custom-call | flops 15703474176 | bytes 12582912 | tf_op jit(solution)/shard_map/nets_second_half_transport/pallas_call | solution.py:257
Async XLA Ops:
  0.6 7.1 %copy-start = (f32[96,48,256]{2,1,0:T(8,128)S(1)}, f32[96,48,256]{2,1,0:T(8,128)}, u32[]{:S(2)}) copy-start(f32[96,48,256]{2,1,0:T(8,128)} %state.5) | copy-start | bytes 14155780
  0.6 7.1 %copy-start.1 = (bf16[2,1024,1024]{2,1,0:T(8,128)(2,1)S(1)}, bf16[2,1024,1024]{2,1,0:T(8,128)(2,1)}, u32[]{:S(2)}) copy-start(bf16[2,1024,1024]{2,1,0:T(8,128)(2,1)} %short_mid.1) | copy-start | bytes 12582916
  0.7 7.1 %copy-start.3 = (bf16[256,1024]{1,0:T(8,128)(2,1)S(1)}, bf16[256,1024]{1,0:T(8,128)(2,1)}, u32[]{:S(2)}) copy-start(bf16[256,1024]{1,0:T(8,128)(2,1)} %long_in.1) | copy-start | bytes 1572868
  0.7 7.1 %copy-start.4 = (bf16[1024,256]{1,0:T(8,128)(2,1)S(1)}, bf16[1024,256]{1,0:T(8,128)(2,1)}, u32[]{:S(2)}) copy-start(bf16[1024,256]{1,0:T(8,128)(2,1)} %long_out.1) | copy-start | bytes 1572868
  0.7 7.1 %copy-start.5 = (bf16[256,1024]{1,0:T(8,128)(2,1)S(1)}, bf16[256,1024]{1,0:T(8,128)(2,1)}, u32[]{:S(2)}) copy-start(bf16[256,1024]{1,0:T(8,128)(2,1)} %short_in.1) | copy-start | bytes 1572868
  0.7 7.1 %copy-start.6 = (bf16[1024,256]{1,0:T(8,128)(2,1)S(1)}, bf16[1024,256]{1,0:T(8,128)(2,1)}, u32[]{:S(2)}) copy-start(bf16[1024,256]{1,0:T(8,128)(2,1)} %short_out.1) | copy-start | bytes 1572868
  0.7 7.1 %copy-start.7 = (s32[96,48]{0,1:T(8,128)S(1)}, s32[96,48]{0,1:T(8,128)}, u32[]{:S(2)}) copy-start(s32[96,48]{0,1:T(8,128)} %param.12) | copy-start | bytes 55300
  0.7 7.1 %copy-start.8 = (f32[96,48]{0,1:T(8,128)S(1)}, f32[96,48]{0,1:T(8,128)}, u32[]{:S(2)}) copy-start(f32[96,48]{0,1:T(8,128)} %param.13) | copy-start | bytes 55300
  2.2 22.1 %collective-permute-start = (bf16[96,512]{1,0:T(8,128)(2,1)S(1)}, bf16[96,512]{1,0:T(8,128)(2,1)S(1)}, u32[]{:S(2)}, u32[]{:S(2)}) collective-permute-start(bf16[96,512]{1,0:T(8,128)(2,1)S(1)} %get-tuple-element.9), channel_id=1, source_target_pairs={{0,15},{1,2},{2,1},{3,4},{4,3},{5,6},{6,5},{7,8},{8,7},{9,10},{10,... | collective-permute-start | bytes 294920 | tf_op jit(solution)/shard_map/ppermute | solution.py:227
  7.7 16.6 %collective-permute-start.1 = (bf16[96,512]{1,0:T(8,128)(2,1)S(1)}, bf16[96,512]{1,0:T(8,128)(2,1)S(1)}, u32[]{:S(2)}, u32[]{:S(2)}) collective-permute-start(bf16[96,512]{1,0:T(8,128)(2,1)S(1)} %get-tuple-element.10), channel_id=1, source_target_pairs={{0,1},{1,0},{2,3},{3,2},{4,5},{5,4},{6,7},{7,6},{8,9},{9,8},{10,11... | collective-permute-start | bytes 294920 | tf_op jit(solution)/shard_map/ppermute | solution.py:228
  7.8 16.5 %copy-start.2 = (f32[96,48,128]{2,1,0:T(8,128)S(1)}, f32[96,48,128]{2,1,0:T(8,128)}, u32[]{:S(2)}) copy-start(f32[96,48,128]{2,1,0:T(8,128)} %courant.3) | copy-start | bytes 7077892

commit v7 on v6

--- a/solution.py
+++ b/solution.py
@@ -127,7 +127,7 @@
     new_state, tend, prov, edges, west_wind,
 ):
     i = pl.program_id(0)
-    tiles = pl.num_programs(0) - 1
+    tiles = pl.num_programs(0)
     half = tiles * rows
     _, cells, feats = state.shape
     cols = rows * cells
@@ -165,7 +165,7 @@
         west_wind[rows:] = sides(hi, rows, slice(feats, end))[0]
 
     def move():
-        lo = pl.multiple_of((i - 1) * rows, rows)
+        lo = pl.multiple_of(i * rows, rows)
         new_state[0] = transport(
             prov_lo[pl.ds(lo, rows)], courant[pl.ds(lo, rows)],
             edges[:rows], west_wind[:rows], edges[2 * rows : 3 * rows],
@@ -175,18 +175,8 @@
             edges[rows : 2 * rows], west_wind[rows:], edges[3 * rows :],
         )
 
-    @pl.when(i == 0)
-    def _():
-        column_nets()
-
-    @pl.when(jnp.logical_and(i > 0, i < tiles))
-    def _():
-        move()
-        column_nets()
-
-    @pl.when(i == tiles)
-    def _():
-        move()
+    column_nets()
+    move()
 
 
 def shards(
@@ -248,19 +238,13 @@
         name="nets_first_half",
     )(v_day, v_sun, v_state, *weights)
 
-    def here(i):
-        return jnp.minimum(i, steps - 1)
-
-    def before(i):
-        return jnp.maximum(i - 1, 0)
-
     new_state, tend = pl.pallas_call(
         functools.partial(second_kernel, rows),
-        grid=(steps + 1,),
+        grid=(steps,),
         in_specs=[in_vmem] * 7 + [in_hbm] + [in_vmem] * 6,
         out_specs=(
-            pl.BlockSpec((2, rows, cells, feats), lambda i: (0, before(i), 0, 0)),
-            pl.BlockSpec((1, rows, cells, feats), lambda i: (1, here(i), 0, 0)),
+            pl.BlockSpec((2, rows, cells, feats), lambda i: (0, i, 0, 0)),
+            pl.BlockSpec((1, rows, cells, feats), lambda i: (1, i, 0, 0)),
         ),
         out_shape=(jax.ShapeDtypeStruct((2, half, cells, feats), F32), tend_shape),
         input_output_aliases={7: 1},

time: 45.1 us -> 45 us (level)
  no operation moved by 1% of the time
where the time goes in v7:
time: 45 us; the launch traced here: 44.8 us
  Pallas kernels  38.5 us (86%)
  starting transfers between devices  5.51 us (12%)
  between operations  0.77 us (2%)
    pallas_call x1, Pallas kernels, shards(): pl.pallas_call(functools.partial(second_kernel, rows), grid=(steps,), in_...  20.5 us
    pallas_call x1, Pallas kernels, shards(): pl.pallas_call(functools.partial(first_kernel, rows), grid=(steps,), in_s...  16.5 us
    ppermute x1, starting transfers between devices, shards(): halo_b = lax.ppermute(edge_b, 'lon', seam)  5.51 us
    pallas_call x1, Pallas kernels, shards(): pl.pallas_call(pack_kernel, in_specs=[in_hbm] * 5, out_specs=(in_vmem,) *...  1.49 us
  transfers between devices with their start and end apart: 2, of which 0 were waited for; matrix products, arithmetic and copies ran while one was open for 0% of the time, Pallas kernels for 37%

profile of v7, /device:TPU:0, one launch (start us, length us, event | category | flops | bytes accessed | tf_op | source)
XLA Modules:
  0.0 44.8 jit_solution(11882811627246782823)
XLA Ops:
  0.6 0.0 copy-start
  0.6 0.0 copy-start.1
  0.7 0.0 copy-start.3
  0.7 0.0 copy-start.4
  0.7 0.0 copy-start.5
  0.7 0.0 copy-start.6
  0.7 0.0 copy-start.7
  0.7 0.0 copy-start.8
  0.7 1.5 %edges_packed.1 = (bf16[96,512]{1,0:T(8,128)(2,1)S(1)}, bf16[96,512]{1,0:T(8,128)(2,1)S(1)}, f32[1,1024]{1,0:T(1,128)S(1)}) custom-call(s32[48,96]{1,0:T(8,128)} %bitcast.4, f32[48,96]{1,0:T(8,128)} %bitcast.7, bf16[1024]{0:T(1024)(128)(2,1)} %short_sun_hbm.1, f32[96,48,256]{2,1,0:T(8,128)} %state.5, f32[96,48,128]{2,1,0:T(8,128)} %courant.3), custom_call_target="tpu_custom_call" | custom-call | flops 8000000000 | bytes 8388608 | tf_op jit(solution)/shard_map/edges_packed/pallas_call | solution.py:197
  2.2 5.5 %collective-permute-start = (bf16[96,512]{1,0:T(8,128)(2,1)S(1)}, bf16[96,512]{1,0:T(8,128)(2,1)S(1)}, u32[]{:S(2)}, u32[]{:S(2)}) collective-permute-start(bf16[96,512]{1,0:T(8,128)(2,1)S(1)} %get-tuple-element.9), channel_id=1, source_target_pairs={{0,15},{1,2},{2,1},{3,4},{4,3},{5,6},{6,5},{7,8},{8,7},{9,10},{10,... | collective-permute-start | bytes 294920 | tf_op jit(solution)/shard_map/ppermute | solution.py:217
  7.7 0.0 collective-permute-start.1
  7.7 0.0 copy-done
  7.7 0.0 copy-done.1
  7.7 0.0 copy-done.3
  7.7 0.0 copy-done.4
  7.8 0.0 copy-done.5
  7.8 0.0 copy-done.6
  7.8 0.0 copy-done.7
  7.8 0.0 copy-done.8
  7.8 0.0 copy-start.2
  7.8 16.5 %nets_first_half.1 = (bf16[2,48,48,256]{3,2,1,0:T(8,128)(2,1)}, f32[48,48,256]{2,1,0:T(8,128)S(1)}) custom-call(s32[48,96]{1,0:T(8,128)S(1)} %bitcast.5, f32[48,96]{1,0:T(8,128)S(1)} %bitcast.8, f32[96,48,256]{2,1,0:T(8,128)S(1)} %copy-done, bf16[256,1024]{1,0:T(8,128)(2,1)S(1)} %copy-done.3, bf16[1024,256]{1,0:T(8,128)(2,1)S(1)} %copy-done.4, ...), custom_call_target="tpu_custom_call" | custom-call | flops 14495514624 | bytes 2097152 | tf_op jit(solution)/shard_map/nets_first_half/pallas_call | solution.py:228
  24.3 0.0 collective-permute-done.halo_b
  24.3 0.0 collective-permute-done.1.halo_a
  24.3 0.0 copy-done.2
  24.3 20.5 %nets_second_half_transport.1 = (f32[2,48,48,256]{3,2,1,0:T(8,128)}, bf16[2,48,48,256]{3,2,1,0:T(8,128)(2,1)}) custom-call(s32[48,96]{1,0:T(8,128)S(1)} %bitcast.6, f32[48,96]{1,0:T(8,128)S(1)} %bitcast.9, f32[96,48,256]{2,1,0:T(8,128)S(1)} %copy-done, f32[96,48,128]{2,1,0:T(8,128)S(1)} %copy-done.2, ...), custom_call_target="tpu_custom_call", output_to_operand_aliasing={{1}: (7, {})} | custom-call | flops 15703474176 | bytes 12582912 | tf_op jit(solution)/shard_map/nets_second_half_transport/pallas_call | solution.py:241
Async XLA Ops:
  0.6 7.1 %copy-start = (f32[96,48,256]{2,1,0:T(8,128)S(1)}, f32[96,48,256]{2,1,0:T(8,128)}, u32[]{:S(2)}) copy-start(f32[96,48,256]{2,1,0:T(8,128)} %state.5) | copy-start | bytes 14155780
  0.6 7.1 %copy-start.1 = (bf16[2,1024,1024]{2,1,0:T(8,128)(2,1)S(1)}, bf16[2,1024,1024]{2,1,0:T(8,128)(2,1)}, u32[]{:S(2)}) copy-start(bf16[2,1024,1024]{2,1,0:T(8,128)(2,1)} %short_mid.1) | copy-start | bytes 12582916
  0.7 7.1 %copy-start.3 = (bf16[256,1024]{1,0:T(8,128)(2,1)S(1)}, bf16[256,1024]{1,0:T(8,128)(2,1)}, u32[]{:S(2)}) copy-start(bf16[256,1024]{1,0:T(8,128)(2,1)} %long_in.1) | copy-start | bytes 1572868
  0.7 7.1 %copy-start.4 = (bf16[1024,256]{1,0:T(8,128)(2,1)S(1)}, bf16[1024,256]{1,0:T(8,128)(2,1)}, u32[]{:S(2)}) copy-start(bf16[1024,256]{1,0:T(8,128)(2,1)} %long_out.1) | copy-start | bytes 1572868
  0.7 7.1 %copy-start.5 = (bf16[256,1024]{1,0:T(8,128)(2,1)S(1)}, bf16[256,1024]{1,0:T(8,128)(2,1)}, u32[]{:S(2)}) copy-start(bf16[256,1024]{1,0:T(8,128)(2,1)} %short_in.1) | copy-start | bytes 1572868
  0.7 7.1 %copy-start.6 = (bf16[1024,256]{1,0:T(8,128)(2,1)S(1)}, bf16[1024,256]{1,0:T(8,128)(2,1)}, u32[]{:S(2)}) copy-start(bf16[1024,256]{1,0:T(8,128)(2,1)} %short_out.1) | copy-start | bytes 1572868
  0.7 7.1 %copy-start.7 = (s32[96,48]{0,1:T(8,128)S(1)}, s32[96,48]{0,1:T(8,128)}, u32[]{:S(2)}) copy-start(s32[96,48]{0,1:T(8,128)} %param.12) | copy-start | bytes 55300
  0.7 7.1 %copy-start.8 = (f32[96,48]{0,1:T(8,128)S(1)}, f32[96,48]{0,1:T(8,128)}, u32[]{:S(2)}) copy-start(f32[96,48]{0,1:T(8,128)} %param.13) | copy-start | bytes 55300
  2.2 22.1 %collective-permute-start = (bf16[96,512]{1,0:T(8,128)(2,1)S(1)}, bf16[96,512]{1,0:T(8,128)(2,1)S(1)}, u32[]{:S(2)}, u32[]{:S(2)}) collective-permute-start(bf16[96,512]{1,0:T(8,128)(2,1)S(1)} %get-tuple-element.9), channel_id=1, source_target_pairs={{0,15},{1,2},{2,1},{3,4},{4,3},{5,6},{6,5},{7,8},{8,7},{9,10},{10,... | collective-permute-start | bytes 294920 | tf_op jit(solution)/shard_map/ppermute | solution.py:217
  7.7 16.6 %collective-permute-start.1 = (bf16[96,512]{1,0:T(8,128)(2,1)S(1)}, bf16[96,512]{1,0:T(8,128)(2,1)S(1)}, u32[]{:S(2)}, u32[]{:S(2)}) collective-permute-start(bf16[96,512]{1,0:T(8,128)(2,1)S(1)} %get-tuple-element.10), channel_id=1, source_target_pairs={{0,1},{1,0},{2,3},{3,2},{4,5},{5,4},{6,7},{7,6},{8,9},{9,8},{10,11... | collective-permute-start | bytes 294920 | tf_op jit(solution)/shard_map/ppermute | solution.py:218
  7.8 16.5 %copy-start.2 = (f32[96,48,128]{2,1,0:T(8,128)S(1)}, f32[96,48,128]{2,1,0:T(8,128)}, u32[]{:S(2)}) copy-start(f32[96,48,128]{2,1,0:T(8,128)} %courant.3) | copy-start | bytes 7077892

commit v8 on v6

--- a/solution.py
+++ b/solution.py
@@ -26,8 +26,8 @@
     first = silu_of_twice(dot(half_cols, short_in[...]) + half_sun * sun_row)
     hidden = silu_of_twice(dot(half_cols, long_in[...]))
     second = silu_of_twice(dot(first, short_mid[0]) * 0.5)
+    third = silu_of_twice(dot(second, short_mid[1]) * 0.5)
     long_tend = dot(hidden, long_out[...])
-    third = silu_of_twice(dot(second, short_mid[1]) * 0.5)
     short_tend = dot(third, short_out[...])
     return long_tend + jnp.where(sun_col > 0.0, short_tend, 0.0)
 

time: 45.1 us -> 45.1 us (level)
  no operation moved by 1% of the time
where the time goes in v8:
time: 45.1 us; the launch traced here: 44.9 us
  Pallas kernels  38.6 us (86%)
  starting transfers between devices  5.51 us (12%)
  between operations  0.77 us (2%)
    pallas_call x1, Pallas kernels, shards(): pl.pallas_call(functools.partial(second_kernel, rows), grid=(steps + 1,),...  20.6 us
    pallas_call x1, Pallas kernels, shards(): pl.pallas_call(functools.partial(first_kernel, rows), grid=(steps,), in_s...  16.5 us
    ppermute x1, starting transfers between devices, shards(): halo_b = lax.ppermute(edge_b, 'lon', seam)  5.51 us
    pallas_call x1, Pallas kernels, shards(): pl.pallas_call(pack_kernel, in_specs=[in_hbm] * 5, out_specs=(in_vmem,) *...  1.49 us
  transfers between devices with their start and end apart: 2, of which 0 were waited for; matrix products, arithmetic and copies ran while one was open for 0% of the time, Pallas kernels for 37%

profile of v8, /device:TPU:0, one launch (start us, length us, event | category | flops | bytes accessed | tf_op | source)
XLA Modules:
  0.0 44.9 jit_solution(4875690706509162738)
XLA Ops:
  0.6 0.0 copy-start
  0.6 0.0 copy-start.1
  0.7 0.0 copy-start.3
  0.7 0.0 copy-start.4
  0.7 0.0 copy-start.5
  0.7 0.0 copy-start.6
  0.7 0.0 copy-start.7
  0.7 0.0 copy-start.8
  0.7 1.5 %edges_packed.1 = (bf16[96,512]{1,0:T(8,128)(2,1)S(1)}, bf16[96,512]{1,0:T(8,128)(2,1)S(1)}, f32[1,1024]{1,0:T(1,128)S(1)}) custom-call(s32[48,96]{1,0:T(8,128)} %bitcast.4, f32[48,96]{1,0:T(8,128)} %bitcast.7, bf16[1024]{0:T(1024)(128)(2,1)} %short_sun_hbm.1, f32[96,48,256]{2,1,0:T(8,128)} %state.5, f32[96,48,128]{2,1,0:T(8,128)} %courant.3), custom_call_target="tpu_custom_call" | custom-call | flops 8000000000 | bytes 8388608 | tf_op jit(solution)/shard_map/edges_packed/pallas_call | solution.py:207
  2.2 5.5 %collective-permute-start = (bf16[96,512]{1,0:T(8,128)(2,1)S(1)}, bf16[96,512]{1,0:T(8,128)(2,1)S(1)}, u32[]{:S(2)}, u32[]{:S(2)}) collective-permute-start(bf16[96,512]{1,0:T(8,128)(2,1)S(1)} %get-tuple-element.9), channel_id=1, source_target_pairs={{0,15},{1,2},{2,1},{3,4},{4,3},{5,6},{6,5},{7,8},{8,7},{9,10},{10,... | collective-permute-start | bytes 294920 | tf_op jit(solution)/shard_map/ppermute | solution.py:227
  7.7 0.0 collective-permute-start.1
  7.7 0.0 copy-done
  7.7 0.0 copy-done.1
  7.7 0.0 copy-done.3
  7.7 0.0 copy-done.4
  7.8 0.0 copy-done.5
  7.8 0.0 copy-done.6
  7.8 0.0 copy-done.7
  7.8 0.0 copy-done.8
  7.8 0.0 copy-start.2
  7.8 16.5 %nets_first_half.1 = (bf16[2,48,48,256]{3,2,1,0:T(8,128)(2,1)}, f32[48,48,256]{2,1,0:T(8,128)S(1)}) custom-call(s32[48,96]{1,0:T(8,128)S(1)} %bitcast.5, f32[48,96]{1,0:T(8,128)S(1)} %bitcast.8, f32[96,48,256]{2,1,0:T(8,128)S(1)} %copy-done, bf16[256,1024]{1,0:T(8,128)(2,1)S(1)} %copy-done.3, bf16[1024,256]{1,0:T(8,128)(2,1)S(1)} %copy-done.4, ...), custom_call_target="tpu_custom_call" | custom-call | flops 14495514624 | bytes 2097152 | tf_op jit(solution)/shard_map/nets_first_half/pallas_call | solution.py:238
  24.3 0.0 collective-permute-done.halo_b
  24.3 0.0 collective-permute-done.1.halo_a
  24.3 0.0 copy-done.2
  24.3 20.6 %nets_second_half_transport.1 = (f32[2,48,48,256]{3,2,1,0:T(8,128)}, bf16[2,48,48,256]{3,2,1,0:T(8,128)(2,1)}) custom-call(s32[48,96]{1,0:T(8,128)S(1)} %bitcast.6, f32[48,96]{1,0:T(8,128)S(1)} %bitcast.9, f32[96,48,256]{2,1,0:T(8,128)S(1)} %copy-done, f32[96,48,128]{2,1,0:T(8,128)S(1)} %copy-done.2, ...), custom_call_target="tpu_custom_call", output_to_operand_aliasing={{1}: (7, {})} | custom-call | flops 15703474176 | bytes 12582912 | tf_op jit(solution)/shard_map/nets_second_half_transport/pallas_call | solution.py:257
Async XLA Ops:
  0.6 7.1 %copy-start = (f32[96,48,256]{2,1,0:T(8,128)S(1)}, f32[96,48,256]{2,1,0:T(8,128)}, u32[]{:S(2)}) copy-start(f32[96,48,256]{2,1,0:T(8,128)} %state.5) | copy-start | bytes 14155780
  0.6 7.1 %copy-start.1 = (bf16[2,1024,1024]{2,1,0:T(8,128)(2,1)S(1)}, bf16[2,1024,1024]{2,1,0:T(8,128)(2,1)}, u32[]{:S(2)}) copy-start(bf16[2,1024,1024]{2,1,0:T(8,128)(2,1)} %short_mid.1) | copy-start | bytes 12582916
  0.7 7.1 %copy-start.3 = (bf16[256,1024]{1,0:T(8,128)(2,1)S(1)}, bf16[256,1024]{1,0:T(8,128)(2,1)}, u32[]{:S(2)}) copy-start(bf16[256,1024]{1,0:T(8,128)(2,1)} %long_in.1) | copy-start | bytes 1572868
  0.7 7.1 %copy-start.4 = (bf16[1024,256]{1,0:T(8,128)(2,1)S(1)}, bf16[1024,256]{1,0:T(8,128)(2,1)}, u32[]{:S(2)}) copy-start(bf16[1024,256]{1,0:T(8,128)(2,1)} %long_out.1) | copy-start | bytes 1572868
  0.7 7.1 %copy-start.5 = (bf16[256,1024]{1,0:T(8,128)(2,1)S(1)}, bf16[256,1024]{1,0:T(8,128)(2,1)}, u32[]{:S(2)}) copy-start(bf16[256,1024]{1,0:T(8,128)(2,1)} %short_in.1) | copy-start | bytes 1572868
  0.7 7.1 %copy-start.6 = (bf16[1024,256]{1,0:T(8,128)(2,1)S(1)}, bf16[1024,256]{1,0:T(8,128)(2,1)}, u32[]{:S(2)}) copy-start(bf16[1024,256]{1,0:T(8,128)(2,1)} %short_out.1) | copy-start | bytes 1572868
  0.7 7.1 %copy-start.7 = (s32[96,48]{0,1:T(8,128)S(1)}, s32[96,48]{0,1:T(8,128)}, u32[]{:S(2)}) copy-start(s32[96,48]{0,1:T(8,128)} %param.12) | copy-start | bytes 55300
  0.7 7.1 %copy-start.8 = (f32[96,48]{0,1:T(8,128)S(1)}, f32[96,48]{0,1:T(8,128)}, u32[]{:S(2)}) copy-start(f32[96,48]{0,1:T(8,128)} %param.13) | copy-start | bytes 55300
  2.2 22.1 %collective-permute-start = (bf16[96,512]{1,0:T(8,128)(2,1)S(1)}, bf16[96,512]{1,0:T(8,128)(2,1)S(1)}, u32[]{:S(2)}, u32[]{:S(2)}) collective-permute-start(bf16[96,512]{1,0:T(8,128)(2,1)S(1)} %get-tuple-element.9), channel_id=1, source_target_pairs={{0,15},{1,2},{2,1},{3,4},{4,3},{5,6},{6,5},{7,8},{8,7},{9,10},{10,... | collective-permute-start | bytes 294920 | tf_op jit(solution)/shard_map/ppermute | solution.py:227
  7.7 16.6 %collective-permute-start.1 = (bf16[96,512]{1,0:T(8,128)(2,1)S(1)}, bf16[96,512]{1,0:T(8,128)(2,1)S(1)}, u32[]{:S(2)}, u32[]{:S(2)}) collective-permute-start(bf16[96,512]{1,0:T(8,128)(2,1)S(1)} %get-tuple-element.10), channel_id=1, source_target_pairs={{0,1},{1,0},{2,3},{3,2},{4,5},{5,4},{6,7},{7,6},{8,9},{9,8},{10,11... | collective-permute-start | bytes 294920 | tf_op jit(solution)/shard_map/ppermute | solution.py:228
  7.8 16.5 %copy-start.2 = (f32[96,48,128]{2,1,0:T(8,128)S(1)}, f32[96,48,128]{2,1,0:T(8,128)}, u32[]{:S(2)}) copy-start(f32[96,48,128]{2,1,0:T(8,128)} %courant.3) | copy-start | bytes 7077892
